TPU v7x, 512 devices: a whole 4x4x16 slice. The times are simulated.
512 devices in a mesh: leaf: 256 (over z, x, y), vec: 2 (over core).
Axes of the slice: x: 4, y: 4, z: 16, core: 2. Of those that a mesh axis runs over, the one named last changes fastest.
Arguments:
- vectors: float32 [256, 524288], P('vec', 'leaf'), may hold values from -6 to 6
- points: bfloat16 [3, 524288], P(None, 'leaf'), may hold values from 0 to 1
- basis: bfloat16 [524288, 128], P('leaf'), may hold values from -0.25 to 0.25
- near_list: int32 [1024, 7], P('leaf'), may hold values from -1 to 1023, as said below
- transfer_leaf: bfloat16 [131072, 128], P('leaf'), may hold values from -0.5 to 0.5
- transfer_one: bfloat16 [65536, 128], P('leaf'), may hold values from -0.5 to 0.5
- transfer_two: bfloat16 [32768, 128], P('leaf'), may hold values from -0.5 to 0.5
- transfer_three: bfloat16 [16384, 128], P('leaf'), may hold values from -0.5 to 0.5
- couple_zero: bfloat16 [4096, 128, 128], P('leaf'), as said below
- couple_one: bfloat16 [2048, 128, 128], P('leaf'), as said below
- couple_two: bfloat16 [1024, 128, 128], P('leaf'), as said below
- couple_three: bfloat16 [512, 128, 128], P('leaf'), as said below
- couple_four: bfloat16 [256, 128, 128], P('leaf'), as said below
Outputs:
- products: float32 [256, 524288], P('vec', 'leaf')
Inputs may be any that keep to these rules, and one draw needn't show every extreme that they name: `near_list`: row l holds leaf l and, in any order and without repeats, some of the leaves l - 3 to l + 3 other than l; every other entry is -1. A row l that is a multiple of 4 holds every leaf from l - 3 to l + 3 that lies in 0 to 1023. `couple_zero`: A block 4 t + j whose cluster t + o_j lies outside the level is zero. `couple_one`: Likewise. `couple_two`: Likewise. `couple_three`: Likewise. `couple_four`: Likewise.
All inputs are finite; a program needn't handle non-finite values.
Results may differ from a plain program's by a relative error of at most 0.013.
Values may be sent and summed in bfloat16 or wider, within the bound.
A program may use at most 64 MiB of HBM per device.

v0:
```python
import jax
import jax.numpy as jnp
from jax import lax
from jax.sharding import PartitionSpec as P

sharpness = 40.0
offsets = (-3, -2, 2, 3)


def swapped(value, axis, distance):
    return lax.ppermute(value, axis, [(i, i ^ 1 << distance) for i in range(lax.axis_size(axis))])


def from_behind(value, axis, by):
    length = lax.axis_size(axis)
    pairs = [(i, i + by) for i in range(length) if 0 <= i + by < length]
    return lax.ppermute(value, axis, pairs)


def with_halo(value, sides, width):
    for axis, dim in sides:
        size, length = (lax.axis_size(axis), value.shape[dim])
        up = [(i, (i + 1) % size) for i in range(size - 1)]
        down = [(j, i) for i, j in up]
        last = lax.slice_in_dim(value, length - width, length, axis=dim)
        first = lax.slice_in_dim(value, 0, width, axis=dim)
        before = lax.ppermute(last, axis, up)
        after = lax.ppermute(first, axis, down)
        value = jnp.concatenate([before, value, after], axis=dim)
    return value


def kernel_blocks(target, sources, live_mask):
    distance = (target[0][None, :, None] - sources[0][:, None, :]) ** 2
    distance = distance + (target[1][None, :, None] - sources[1][:, None, :]) ** 2
    distance = distance + (target[2][None, :, None] - sources[2][:, None, :]) ** 2
    return (jnp.exp(-sharpness * distance) * live_mask[:, None, None]).astype(jnp.bfloat16)


def partner(values, bit_pos):
    return swapped(values, "leaf", bit_pos)


def span_total(values, bit_count):
    for bit_pos in range(bit_count):
        values = values + partner(values, bit_pos)
    return values


def neighbour(values, move_by):
    return from_behind(values, "leaf", -move_by)


def level_neighbour(values, move_by):
    if move_by == 0:
        return values
    return from_behind(values, "leaf", -move_by)


def couple_local(low_level, blocks, fetch_owner):
    cluster_count, rank_size, local_vecs = low_level.shape
    fetched = {}
    sources = []
    for cluster in range(cluster_count):
        for move_by in offsets:
            spot_pos = cluster + move_by
            owner_dev = spot_pos // cluster_count
            if owner_dev not in fetched:
                fetched[owner_dev] = fetch_owner(owner_dev)
            sources.append(fetched[owner_dev][spot_pos % cluster_count])
    stacked = jnp.stack(sources)
    summands = jnp.einsum("brs,bsv->brv", blocks, stacked, preferred_element_type=jnp.float32)
    return summands.reshape(cluster_count, 4, rank_size, local_vecs).sum(1)


def couple_upper(low_level, blocks, span_size):
    stacked = jnp.stack([neighbour(low_level, move_by * span_size) for move_by in offsets])
    block_count = blocks.shape[0]
    first_slot = lax.axis_index("leaf") % (4 // block_count) * block_count
    my_sources = lax.dynamic_slice_in_dim(stacked, first_slot, block_count, 0)
    summands = jnp.einsum("brs,bsv->rv", blocks, my_sources, preferred_element_type=jnp.float32)
    return span_total(summands, span_size.bit_length() - 1)


def climb(low_level, transfer, rank_size):
    matrices = transfer.reshape(-1, rank_size, rank_size)
    summands = jnp.einsum("lrs,lrv->lsv", matrices, low_level, preferred_element_type=jnp.float32)
    return summands.reshape(-1, 2, rank_size, low_level.shape[2]).sum(1)


def descend(far_level, transfer, parent_low, rank_size):
    matrices = transfer.reshape(-1, rank_size, rank_size)
    parents = jnp.repeat(parent_low, 2, axis=0)
    return far_level + jnp.einsum(
        "lrs,lsv->lrv", matrices, parents, preferred_element_type=jnp.float32
    )


def body(
    vectors,
    points,
    basis,
    near_list,
    transfer_leaf,
    transfer_one,
    transfer_two,
    transfer_three,
    couple_zero,
    couple_one,
    couple_two,
    couple_three,
    couple_four,
):
    local_vecs, point_count = vectors.shape
    leaf_count = near_list.shape[0]
    leaf_size = point_count // leaf_count
    rank_size = basis.shape[1]
    leaf_index = lax.axis_index("leaf")
    vec_low = vectors.astype(jnp.bfloat16)
    packed = jnp.concatenate([vec_low, points], axis=0)
    window = with_halo(packed, (("leaf", 1),), 3 * leaf_size)
    window_vec = window[:local_vecs]
    window_span = leaf_count + 6
    window_pts = window[local_vecs:].astype(jnp.float32).reshape(3, window_span, leaf_size)
    window_base = leaf_index * leaf_count - 3
    leaf_share = leaf_count // lax.axis_size("vec")
    first_leaf = lax.axis_index("vec") * leaf_share
    tiles_tile_list = []
    tiles_slot_list = []
    for position in range(leaf_share):
        leaf_pos = first_leaf + position
        listed = lax.dynamic_index_in_dim(near_list, leaf_pos, 0, keepdims=False)
        slot_pos = jnp.clip(listed - window_base, 0, window_span - 1)
        live_mask = (listed >= 0).astype(jnp.float32)
        target = lax.dynamic_slice_in_dim(points, leaf_pos * leaf_size, leaf_size, 1).astype(
            jnp.float32
        )
        sources = jnp.take(window_pts, slot_pos, axis=1)
        tiles_tile_list.append(kernel_blocks(target, sources, live_mask))
        tiles_slot_list.append(slot_pos)
    vec_window = lax.all_gather(window_vec, "vec", axis=0, tiled=True)
    row_count = vec_window.shape[0]
    vec_grid = vec_window.reshape(row_count, window_span, leaf_size)
    results = []
    for tiles, slot_pos in zip(tiles_tile_list, tiles_slot_list):
        picked = jnp.take(vec_grid, slot_pos, axis=1)
        results.append(jnp.einsum("vmq,mpq->vp", picked, tiles, preferred_element_type=jnp.float32))
    near_mixed = jnp.concatenate(results, axis=1)
    near_field = lax.all_to_all(
        near_mixed.astype(jnp.bfloat16), "vec", split_axis=0, concat_axis=1, tiled=True
    ).astype(near_mixed.dtype)
    basis_grid = basis.reshape(leaf_count, leaf_size, rank_size)
    leaf_coef = jnp.einsum(
        "lpr,vlp->lrv",
        basis_grid,
        vec_low.reshape(local_vecs, leaf_count, leaf_size),
        preferred_element_type=jnp.float32,
    )
    low_zero = leaf_coef.astype(jnp.bfloat16)
    low_one = climb(low_zero, transfer_leaf, rank_size).astype(jnp.bfloat16)
    low_two = climb(low_one, transfer_one, rank_size).astype(jnp.bfloat16)
    partial_three = jnp.einsum(
        "rs,rv->sv", transfer_two, low_two[0], preferred_element_type=jnp.float32
    )
    low_three = span_total(partial_three, 1).astype(jnp.bfloat16)
    half_rank = rank_size // 2
    row_start = leaf_index % 2 * half_rank
    rows_three = lax.dynamic_slice_in_dim(low_three, row_start, half_rank, 0)
    partial_four = jnp.einsum(
        "rs,rv->sv", transfer_three, rows_three, preferred_element_type=jnp.float32
    )
    low_four = span_total(partial_four, 2).astype(jnp.bfloat16)
    far_zero = couple_local(
        low_zero, couple_zero, lambda owner_dev: level_neighbour(low_zero, owner_dev)
    )
    far_one = couple_local(
        low_one, couple_one, lambda owner_dev: level_neighbour(low_one, owner_dev)
    )
    far_two = couple_local(
        low_two, couple_two, lambda owner_dev: level_neighbour(low_two, owner_dev)
    )
    far_three = couple_upper(low_three, couple_three, 2)
    far_four = couple_upper(low_four, couple_four, 4)
    down_four = far_four.astype(jnp.bfloat16)
    own_rows = jnp.einsum(
        "rs,sv->rv", transfer_three, down_four, preferred_element_type=jnp.float32
    )
    peer_rows = partner(own_rows, 0)
    joined = jnp.where(
        leaf_index % 2 == 0,
        jnp.concatenate([own_rows, peer_rows], axis=0),
        jnp.concatenate([peer_rows, own_rows], axis=0),
    )
    down_three = (far_three + joined).astype(jnp.bfloat16)
    down_two = (
        far_two[0]
        + jnp.einsum("rs,sv->rv", transfer_two, down_three, preferred_element_type=jnp.float32)
    ).astype(jnp.bfloat16)[None]
    down_one = descend(far_one, transfer_one, down_two, rank_size).astype(jnp.bfloat16)
    down_zero = descend(far_zero, transfer_leaf, down_one, rank_size).astype(jnp.bfloat16)
    far_field = jnp.einsum(
        "lpr,lrv->vlp", basis_grid, down_zero, preferred_element_type=jnp.float32
    ).reshape(local_vecs, point_count)
    return near_field + far_field


def solution(mesh):
    placed = (
        P("vec", "leaf"),
        P(None, "leaf"),
        P("leaf", None),
        P("leaf", None),
        P("leaf", None),
        P("leaf", None),
        P("leaf", None),
        P("leaf", None),
        P("leaf", None, None),
        P("leaf", None, None),
        P("leaf", None, None),
        P("leaf", None, None),
        P("leaf", None, None),
    )
    return jax.shard_map(
        body, mesh=mesh, in_specs=placed, out_specs=P("vec", "leaf"), check_vma=False
    )
```

profile of v0, /device:TPU:1, one launch (start us, length us, event | category | flops | bytes accessed | tf_op | source)
XLA Modules:
  0.0 188.8 jit_solution(2352364276355460504)
XLA Ops:
  8.6 4.0 %collective-permute-start.5 = (bf16[2,128,128]{1,2,0:T(8,128)(2,1)S(1)}, bf16[2,128,128]{1,2,0:T(8,128)(2,1)S(1)}, u32[]{:S(2)}, u32[]{:S(2)}) collective-permute-start(bf16[2,128,128]{1,2,0:T(8,128)(2,1)S(1)} %bitcast_reduce_fusion.2), channel_id=1, source_target_pairs={{0,2},{2,4},{4,6},{6,8},{8,10},{10,12},{12,14},{14,16},{16,18},{18... | collective-permute-start | bytes 196616 | tf_op jit(solution)/shard_map/ppermute | solution.py:17
  12.7 4.5 %collective-permute-start.4 = (bf16[2,128,128]{1,2,0:T(8,128)(2,1)S(1)}, bf16[2,128,128]{1,2,0:T(8,128)(2,1)S(1)}, u32[]{:S(2)}, u32[]{:S(2)}) collective-permute-start(bf16[2,128,128]{1,2,0:T(8,128)(2,1)S(1)} %bitcast_reduce_fusion.2), channel_id=1, source_target_pairs={{0,4},{2,6},{4,8},{6,10},{8,12},{10,14},{12,16},{14,18},{16,20},{1... | collective-permute-start | bytes 196616 | tf_op jit(solution)/shard_map/ppermute | solution.py:17
  20.2 4.0 %collective-permute-start.12 = (f32[128,128]{1,0:T(8,128)S(1)}, f32[128,128]{1,0:T(8,128)S(1)}, u32[]{:S(2)}, u32[]{:S(2)}) collective-permute-start(f32[128,128]{1,0:T(8,128)S(1)} %convolution_bitcast_fusion.7), channel_id=1, source_target_pairs={{0,2},{2,0},{4,6},{6,4},{8,10},{10,8},{12,14},{14,12},{16,18},{18,... | collective-permute-start | bytes 196616 | tf_op jit(solution)/shard_map/ppermute | solution.py:11
  26.8 3.0 %collective-permute-start.2 = (bf16[4,128,128]{2,1,0:T(8,128)(2,1)S(1)}, bf16[4,128,128]{2,1,0:T(8,128)(2,1)S(1)}, u32[]{:S(2)}, u32[]{:S(2)}) collective-permute-start(bf16[4,128,128]{2,1,0:T(8,128)(2,1)S(1)} %convolution_convert_fusion), channel_id=1, source_target_pairs={{0,2},{2,4},{4,6},{6,8},{8,10},{10,12},{12,14},{14,16},{16,18},{18... | collective-permute-start | bytes 393224 | tf_op jit(solution)/shard_map/ppermute | solution.py:17
  30.0 6.9 %collective-permute-start.13 = (bf16[128,128]{1,0:T(8,128)(2,1)S(1)}, bf16[128,128]{1,0:T(8,128)(2,1)S(1)}, u32[]{:S(2)}, u32[]{:S(2)}) collective-permute-start(bf16[128,128]{1,0:T(8,128)(2,1)S(1)} %add_convert_fusion.2), channel_id=1, source_target_pairs={{0,12},{2,14},{4,16},{6,18},{8,20},{10,22},{12,24},{14,26},{16,28}... | collective-permute-start | bytes 98312 | tf_op jit(solution)/shard_map/ppermute | solution.py:17
  37.0 3.1 %collective-permute-start.14 = (bf16[128,128]{1,0:T(8,128)(2,1)S(1)}, bf16[128,128]{1,0:T(8,128)(2,1)S(1)}, u32[]{:S(2)}, u32[]{:S(2)}) collective-permute-start(bf16[128,128]{1,0:T(8,128)(2,1)S(1)} %add_convert_fusion.2), channel_id=1, source_target_pairs={{0,8},{2,10},{4,12},{6,14},{8,16},{10,18},{12,20},{14,22},{16,24},... | collective-permute-start | bytes 98312 | tf_op jit(solution)/shard_map/ppermute | solution.py:17
  45.7 4.0 %collective-permute-start.18 = (f32[128,128]{0,1:T(8,128)S(1)}, f32[128,128]{0,1:T(8,128)S(1)}, u32[]{:S(2)}, u32[]{:S(2)}) collective-permute-start(f32[128,128]{0,1:T(8,128)S(1)} %convolution_bitcast_fusion.5), channel_id=1, source_target_pairs={{0,2},{2,0},{4,6},{6,4},{8,10},{10,8},{12,14},{14,12},{16,18},{18,... | collective-permute-start | bytes 196616 | tf_op jit(solution)/shard_map/ppermute | solution.py:11
  50.0 2.2 %collective-permute-done.18 = f32[128,128]{0,1:T(8,128)S(1)} collective-permute-done((f32[128,128]{0,1:T(8,128)S(1)}, f32[128,128]{0,1:T(8,128)S(1)}, u32[]{:S(2)}, u32[]{:S(2)}) %collective-permute-start.18) | collective-permute-done | bytes 65568 | tf_op jit(solution)/shard_map/ppermute | solution.py:11
  52.2 5.9 %collective-permute-start.19 = (f32[128,128]{0,1:T(8,128)S(1)}, f32[128,128]{0,1:T(8,128)S(1)}, u32[]{:S(2)}, u32[]{:S(2)}) collective-permute-start(f32[128,128]{0,1:T(8,128)S(1)} %add.103), channel_id=1, source_target_pairs={{0,4},{2,6},{4,0},{6,2},{8,12},{10,14},{12,8},{14,10},{16,20},{18,... | collective-permute-start | bytes 196616 | tf_op jit(solution)/shard_map/ppermute | solution.py:11
  60.4 10.2 %collective-permute-start.20 = (bf16[128,128]{0,1:T(8,128)(2,1)S(1)}, bf16[128,128]{0,1:T(8,128)(2,1)S(1)}, u32[]{:S(2)}, u32[]{:S(2)}) collective-permute-start(bf16[128,128]{0,1:T(8,128)(2,1)S(1)} %add_convert_fusion.1), channel_id=1, source_target_pairs={{0,24},{2,26},{4,28},{6,30},{8,32},{10,34},{12,36},{14,38},{16,40}... | collective-permute-start | bytes 98312 | tf_op jit(solution)/shard_map/ppermute | solution.py:17
  70.6 6.2 %collective-permute-start.21 = (bf16[128,128]{0,1:T(8,128)(2,1)S(1)}, bf16[128,128]{0,1:T(8,128)(2,1)S(1)}, u32[]{:S(2)}, u32[]{:S(2)}) collective-permute-start(bf16[128,128]{0,1:T(8,128)(2,1)S(1)} %add_convert_fusion.1), channel_id=1, source_target_pairs={{0,16},{2,18},{4,20},{6,22},{8,24},{10,26},{12,28},{14,30},{16,32}... | collective-permute-start | bytes 98312 | tf_op jit(solution)/shard_map/ppermute | solution.py:17
  84.4 4.0 %collective-permute-start.24 = (f32[128,128]{0,1:T(8,128)S(1)}, f32[128,128]{0,1:T(8,128)S(1)}, u32[]{:S(2)}, u32[]{:S(2)}) collective-permute-start(f32[128,128]{0,1:T(8,128)S(1)} %convolution_bitcast_fusion.4), channel_id=1, source_target_pairs={{0,2},{2,0},{4,6},{6,4},{8,10},{10,8},{12,14},{14,12},{16,18},{18,... | collective-permute-start | bytes 196616 | tf_op jit(solution)/shard_map/ppermute | solution.py:11
  88.4 4.1 %collective-permute-done.24 = f32[128,128]{0,1:T(8,128)S(1)} collective-permute-done((f32[128,128]{0,1:T(8,128)S(1)}, f32[128,128]{0,1:T(8,128)S(1)}, u32[]{:S(2)}, u32[]{:S(2)}) %collective-permute-start.24) | collective-permute-done | bytes 65568 | tf_op jit(solution)/shard_map/ppermute | solution.py:11
  92.6 5.0 %collective-permute-start.8 = (bf16[1,128,128]{1,2,0:T(8,128)(2,1)S(1)}, bf16[1,128,128]{1,2,0:T(8,128)(2,1)}, u32[]{:S(2)}, u32[]{:S(2)}) collective-permute-start(bf16[1,128,128]{1,2,0:T(8,128)(2,1)S(1)} %bitcast.185), channel_id=1, source_target_pairs={{0,6},{2,8},{4,10},{6,12},{8,14},{10,16},{12,18},{14,20},{16,22},{... | collective-permute-start | bytes 98312 | tf_op jit(solution)/shard_map/ppermute | solution.py:17
  97.5 3.3 %collective-permute-start.17 = (f32[128,128]{0,1:T(8,128)S(1)}, f32[128,128]{0,1:T(8,128)S(1)}, u32[]{:S(2)}, u32[]{:S(2)}) collective-permute-start(f32[128,128]{0,1:T(8,128)S(1)} %convolution_bitcast_fusion.6), channel_id=1, source_target_pairs={{0,2},{2,0},{4,6},{6,4},{8,10},{10,8},{12,14},{14,12},{16,18},{18,... | collective-permute-start | bytes 196616 | tf_op jit(solution)/shard_map/ppermute | solution.py:11
  100.9 4.6 %collective-permute-start.25 = (f32[128,128]{0,1:T(8,128)S(1)}, f32[128,128]{0,1:T(8,128)S(1)}, u32[]{:S(2)}, u32[]{:S(2)}) collective-permute-start(f32[128,128]{0,1:T(8,128)S(1)} %add.107), channel_id=1, source_target_pairs={{0,4},{2,6},{4,0},{6,2},{8,12},{10,14},{12,8},{14,10},{16,20},{18,... | collective-permute-start | bytes 196616 | tf_op jit(solution)/shard_map/ppermute | solution.py:11
  111.1 4.8 %collective-permute-start.9 = (bf16[1,128,128]{1,2,0:T(8,128)(2,1)S(1)}, bf16[1,128,128]{1,2,0:T(8,128)(2,1)S(1)}, u32[]{:S(2)}, u32[]{:S(2)}) collective-permute-start(bf16[1,128,128]{1,2,0:T(8,128)(2,1)S(1)} %bitcast.186), channel_id=1, source_target_pairs={{0,4},{2,6},{4,8},{6,10},{8,12},{10,14},{12,16},{14,18},{16,20},{1... | collective-permute-start | bytes 98312 | tf_op jit(solution)/shard_map/ppermute | solution.py:17
  121.2 30.3 %all-gather.2.cloned.1.call-done = bf16[256,5120]{1,0:T(8,128)(2,1)} async-done(((bf16[128,5120]{1,0:T(8,128)(2,1)}), bf16[256,5120]{1,0:T(8,128)(2,1)}) %all-gather.2.cloned.1.call-update) | async-done | bytes 2621456 | tf_op jit(solution)/shard_map/all_gather | solution.py:141
  151.5 4.4 %copy.59 = bf16[256,5120]{0,1:T(8,128)(2,1)} copy(bf16[256,5120]{1,0:T(8,128)(2,1)} %all-gather.2.cloned.1.call-done) | data formatting | bytes 5242880 | tf_op jit(solution)/shard_map/all_gather | solution.py:141
  156.0 3.0 %copy.60 = bf16[256,10,512]{2,0,1:T(8,128)(2,1)S(1)} copy(bf16[256,10,512]{0,2,1:T(8,128)(2,1)} %bitcast.174) | data formatting | bytes 5242880 | tf_op jit(solution)/shard_map/reshape | solution.py:143
  162.9 5.0 %fusion.14 = bf16[256,512]{1,0:T(8,128)(2,1)S(1)} fusion(f32[7]{0:T(128)S(1)} %copy-done.19, f32[7,512]{1,0:T(8,128)S(1)} %bitcast.191, f32[512]{0:T(512)S(1)} %bitcast.201, f32[7,512]{1,0:T(8,128)S(1)} %bitcast.192, f32[512]{0:T(512)S(1)} %bitcast.202, f32[7,512]{1,0:T(8,128)S(1)} %bitcast.195, f32[512]{0:T(512)S(1)} %bitcast.200, ...), kind=kOutput, calls=%fused_computation.18 | convolution fusion | flops 960757760 | bytes 2146339 | tf_op jit(solution)/shard_map/vmq,mpq->vp/dot_general | solution.py:147
  168.0 3.4 %fusion.17 = bf16[256,512]{1,0:T(8,128)(2,1)S(1)} fusion(f32[7]{0:T(128)S(1)} %copy-done.18, f32[7,512]{1,0:T(8,128)S(1)} %bitcast.193, f32[512]{0:T(512)S(1)} %bitcast.198, f32[7,512]{1,0:T(8,128)S(1)} %bitcast.194, f32[512]{0:T(512)S(1)} %bitcast.197, f32[7,512]{1,0:T(8,128)S(1)} %bitcast.196, f32[512]{0:T(512)S(1)} %bitcast.199, ...), kind=kOutput, calls=%fused_computation.19 | convolution fusion | flops 960757760 | bytes 2146339 | tf_op jit(solution)/shard_map/vmq,mpq->vp/dot_general | solution.py:147
  171.5 4.1 %all_to_all.10 = bf16[2,128,1024]{2,1,0:T(8,128)(2,1)S(1)} all-to-all(bf16[2,128,1024]{2,1,0:T(8,128)(2,1)S(1)} %pad_maximum_fusion.1), channel_id=1, replica_groups=mesh['leaf'=256,'vec'=2] {'vec'}, dimensions={0} | all-to-all | bytes 1048576 | tf_op jit(solution)/shard_map/all_to_all | solution.py:149
  179.4 2.5 %copy.72 = f32[128,2048]{1,0:T(8,128)} copy(f32[128,2048]{0,1:T(8,128)} %bitcast_add_fusion) | data formatting | bytes 2097152 | tf_op jit(solution)/shard_map/add | solution.py:204
  (146 shorter events, 41.9 us)
Async XLA Ops:
  6.6 145.0 %all-gather.2.cloned.1.call-start = ((), (), s32[]{:S(2)}) async-start(), calls=%async_computation.1 | async-start | bytes 3932160 | tf_op jit(solution)/shard_map/all_gather | solution.py:141
  8.6 28.3 %collective-permute-start.5 = (bf16[2,128,128]{1,2,0:T(8,128)(2,1)S(1)}, bf16[2,128,128]{1,2,0:T(8,128)(2,1)S(1)}, u32[]{:S(2)}, u32[]{:S(2)}) collective-permute-start(bf16[2,128,128]{1,2,0:T(8,128)(2,1)S(1)} %bitcast_reduce_fusion.2), channel_id=1, source_target_pairs={{0,2},{2,4},{4,6},{6,8},{8,10},{10,12},{12,14},{14,16},{16,18},{18... | collective-permute-start | bytes 196616 | tf_op jit(solution)/shard_map/ppermute | solution.py:17
  12.7 17.3 %collective-permute-start.4 = (bf16[2,128,128]{1,2,0:T(8,128)(2,1)S(1)}, bf16[2,128,128]{1,2,0:T(8,128)(2,1)S(1)}, u32[]{:S(2)}, u32[]{:S(2)}) collective-permute-start(bf16[2,128,128]{1,2,0:T(8,128)(2,1)S(1)} %bitcast_reduce_fusion.2), channel_id=1, source_target_pairs={{0,4},{2,6},{4,8},{6,10},{8,12},{10,14},{12,16},{14,18},{16,20},{1... | collective-permute-start | bytes 196616 | tf_op jit(solution)/shard_map/ppermute | solution.py:17
  17.2 22.9 %collective-permute-start.6 = (bf16[2,128,128]{1,2,0:T(8,128)(2,1)S(1)}, bf16[2,128,128]{1,2,0:T(8,128)(2,1)S(1)}, u32[]{:S(2)}, u32[]{:S(2)}) collective-permute-start(bf16[2,128,128]{1,2,0:T(8,128)(2,1)S(1)} %bitcast_reduce_fusion.2), channel_id=1, source_target_pairs={{2,0},{4,2},{6,4},{8,6},{10,8},{12,10},{14,12},{16,14},{18,16},{20... | collective-permute-start | bytes 196616 | tf_op jit(solution)/shard_map/ppermute | solution.py:17
  18.5 23.0 %collective-permute-start.7 = (bf16[2,128,128]{1,2,0:T(8,128)(2,1)S(1)}, bf16[2,128,128]{1,2,0:T(8,128)(2,1)S(1)}, u32[]{:S(2)}, u32[]{:S(2)}) collective-permute-start(bf16[2,128,128]{1,2,0:T(8,128)(2,1)S(1)} %bitcast_reduce_fusion.2), channel_id=1, source_target_pairs={{4,0},{6,2},{8,4},{10,6},{12,8},{14,10},{16,12},{18,14},{20,16},{2... | collective-permute-start | bytes 196616 | tf_op jit(solution)/shard_map/ppermute | solution.py:17
  20.2 6.6 %collective-permute-start.12 = (f32[128,128]{1,0:T(8,128)S(1)}, f32[128,128]{1,0:T(8,128)S(1)}, u32[]{:S(2)}, u32[]{:S(2)}) collective-permute-start(f32[128,128]{1,0:T(8,128)S(1)} %convolution_bitcast_fusion.7), channel_id=1, source_target_pairs={{0,2},{2,0},{4,6},{6,4},{8,10},{10,8},{12,14},{14,12},{16,18},{18,... | collective-permute-start | bytes 196616 | tf_op jit(solution)/shard_map/ppermute | solution.py:11
  26.8 31.3 %collective-permute-start.2 = (bf16[4,128,128]{2,1,0:T(8,128)(2,1)S(1)}, bf16[4,128,128]{2,1,0:T(8,128)(2,1)S(1)}, u32[]{:S(2)}, u32[]{:S(2)}) collective-permute-start(bf16[4,128,128]{2,1,0:T(8,128)(2,1)S(1)} %convolution_convert_fusion), channel_id=1, source_target_pairs={{0,2},{2,4},{4,6},{6,8},{8,10},{10,12},{12,14},{14,16},{16,18},{18... | collective-permute-start | bytes 393224 | tf_op jit(solution)/shard_map/ppermute | solution.py:17
  30.0 13.1 %collective-permute-start.13 = (bf16[128,128]{1,0:T(8,128)(2,1)S(1)}, bf16[128,128]{1,0:T(8,128)(2,1)S(1)}, u32[]{:S(2)}, u32[]{:S(2)}) collective-permute-start(bf16[128,128]{1,0:T(8,128)(2,1)S(1)} %add_convert_fusion.2), channel_id=1, source_target_pairs={{0,12},{2,14},{4,16},{6,18},{8,20},{10,22},{12,24},{14,26},{16,28}... | collective-permute-start | bytes 98312 | tf_op jit(solution)/shard_map/ppermute | solution.py:17
  37.0 7.5 %collective-permute-start.14 = (bf16[128,128]{1,0:T(8,128)(2,1)S(1)}, bf16[128,128]{1,0:T(8,128)(2,1)S(1)}, u32[]{:S(2)}, u32[]{:S(2)}) collective-permute-start(bf16[128,128]{1,0:T(8,128)(2,1)S(1)} %add_convert_fusion.2), channel_id=1, source_target_pairs={{0,8},{2,10},{4,12},{6,14},{8,16},{10,18},{12,20},{14,22},{16,24},... | collective-permute-start | bytes 98312 | tf_op jit(solution)/shard_map/ppermute | solution.py:17
  41.5 8.3 %collective-permute-start.16 = (bf16[128,128]{1,0:T(8,128)(2,1)S(1)}, bf16[128,128]{1,0:T(8,128)(2,1)S(1)}, u32[]{:S(2)}, u32[]{:S(2)}) collective-permute-start(bf16[128,128]{1,0:T(8,128)(2,1)S(1)} %add_convert_fusion.2), channel_id=1, source_target_pairs={{12,0},{14,2},{16,4},{18,6},{20,8},{22,10},{24,12},{26,14},{28,16}... | collective-permute-start | bytes 98312 | tf_op jit(solution)/shard_map/ppermute | solution.py:17
  43.1 15.1 %collective-permute-start.3 = (bf16[4,128,128]{2,1,0:T(8,128)(2,1)S(1)}, bf16[4,128,128]{2,1,0:T(8,128)(2,1)S(1)}, u32[]{:S(2)}, u32[]{:S(2)}) collective-permute-start(bf16[4,128,128]{2,1,0:T(8,128)(2,1)S(1)} %convolution_convert_fusion), channel_id=1, source_target_pairs={{2,0},{4,2},{6,4},{8,6},{10,8},{12,10},{14,12},{16,14},{18,16},{20... | collective-permute-start | bytes 393224 | tf_op jit(solution)/shard_map/ppermute | solution.py:17
  44.4 71.7 %collective-permute-start.10 = (bf16[1,128,128]{1,2,0:T(8,128)(2,1)S(1)}, bf16[1,128,128]{1,2,0:T(8,128)(2,1)}, u32[]{:S(2)}, u32[]{:S(2)}) collective-permute-start(bf16[1,128,128]{1,2,0:T(8,128)(2,1)S(1)} %bitcast.183), channel_id=1, source_target_pairs={{4,0},{6,2},{8,4},{10,6},{12,8},{14,10},{16,12},{18,14},{20,16},{2... | collective-permute-start | bytes 98312 | tf_op jit(solution)/shard_map/ppermute | solution.py:17
  45.7 6.5 %collective-permute-start.18 = (f32[128,128]{0,1:T(8,128)S(1)}, f32[128,128]{0,1:T(8,128)S(1)}, u32[]{:S(2)}, u32[]{:S(2)}) collective-permute-start(f32[128,128]{0,1:T(8,128)S(1)} %convolution_bitcast_fusion.5), channel_id=1, source_target_pairs={{0,2},{2,0},{4,6},{6,4},{8,10},{10,8},{12,14},{14,12},{16,18},{18,... | collective-permute-start | bytes 196616 | tf_op jit(solution)/shard_map/ppermute | solution.py:11
  52.2 8.2 %collective-permute-start.19 = (f32[128,128]{0,1:T(8,128)S(1)}, f32[128,128]{0,1:T(8,128)S(1)}, u32[]{:S(2)}, u32[]{:S(2)}) collective-permute-start(f32[128,128]{0,1:T(8,128)S(1)} %add.103), channel_id=1, source_target_pairs={{0,4},{2,6},{4,0},{6,2},{8,12},{10,14},{12,8},{14,10},{16,20},{18,... | collective-permute-start | bytes 196616 | tf_op jit(solution)/shard_map/ppermute | solution.py:11
  60.4 19.0 %collective-permute-start.20 = (bf16[128,128]{0,1:T(8,128)(2,1)S(1)}, bf16[128,128]{0,1:T(8,128)(2,1)S(1)}, u32[]{:S(2)}, u32[]{:S(2)}) collective-permute-start(bf16[128,128]{0,1:T(8,128)(2,1)S(1)} %add_convert_fusion.1), channel_id=1, source_target_pairs={{0,24},{2,26},{4,28},{6,30},{8,32},{10,34},{12,36},{14,38},{16,40}... | collective-permute-start | bytes 98312 | tf_op jit(solution)/shard_map/ppermute | solution.py:17
  70.6 10.1 %collective-permute-start.21 = (bf16[128,128]{0,1:T(8,128)(2,1)S(1)}, bf16[128,128]{0,1:T(8,128)(2,1)S(1)}, u32[]{:S(2)}, u32[]{:S(2)}) collective-permute-start(bf16[128,128]{0,1:T(8,128)(2,1)S(1)} %add_convert_fusion.1), channel_id=1, source_target_pairs={{0,16},{2,18},{4,20},{6,22},{8,24},{10,26},{12,28},{14,30},{16,32}... | collective-permute-start | bytes 98312 | tf_op jit(solution)/shard_map/ppermute | solution.py:17
  79.4 36.7 %collective-permute-start.11 = (bf16[1,128,128]{1,2,0:T(8,128)(2,1)S(1)}, bf16[1,128,128]{1,2,0:T(8,128)(2,1)}, u32[]{:S(2)}, u32[]{:S(2)}) collective-permute-start(bf16[1,128,128]{1,2,0:T(8,128)(2,1)S(1)} %bitcast.184), channel_id=1, source_target_pairs={{6,0},{8,2},{10,4},{12,6},{14,8},{16,10},{18,12},{20,14},{22,16},{... | collective-permute-start | bytes 98312 | tf_op jit(solution)/shard_map/ppermute | solution.py:17
  80.7 16.8 %collective-permute-start = (bf16[131,1536]{1,0:T(8,128)(2,1)}, bf16[131,1536]{1,0:T(8,128)(2,1)S(1)}, u32[]{:S(2)}, u32[]{:S(2)}) collective-permute-start(bf16[131,1536]{1,0:T(8,128)(2,1)} %get-tuple-element.11), channel_id=1, source_target_pairs={{0,2},{2,4},{4,6},{6,8},{8,10},{10,12},{12,14},{14,16},{16,18},{18... | collective-permute-start | bytes 1207304 | tf_op jit(solution)/shard_map/ppermute | solution.py:27
  83.0 17.9 %collective-permute-start.1 = (bf16[131,1536]{1,0:T(8,128)(2,1)S(1)}, bf16[131,1536]{1,0:T(8,128)(2,1)S(1)}, u32[]{:S(2)}, u32[]{:S(2)}) collective-permute-start(bf16[131,1536]{1,0:T(8,128)(2,1)S(1)} %copy-done.4), channel_id=1, source_target_pairs={{2,0},{4,2},{6,4},{8,6},{10,8},{12,10},{14,12},{16,14},{18,16},{20... | collective-permute-start | bytes 1207304 | tf_op jit(solution)/shard_map/ppermute | solution.py:28
  84.4 8.1 %collective-permute-start.24 = (f32[128,128]{0,1:T(8,128)S(1)}, f32[128,128]{0,1:T(8,128)S(1)}, u32[]{:S(2)}, u32[]{:S(2)}) collective-permute-start(f32[128,128]{0,1:T(8,128)S(1)} %convolution_bitcast_fusion.4), channel_id=1, source_target_pairs={{0,2},{2,0},{4,6},{6,4},{8,10},{10,8},{12,14},{14,12},{16,18},{18,... | collective-permute-start | bytes 196616 | tf_op jit(solution)/shard_map/ppermute | solution.py:11
  92.6 23.5 %collective-permute-start.8 = (bf16[1,128,128]{1,2,0:T(8,128)(2,1)S(1)}, bf16[1,128,128]{1,2,0:T(8,128)(2,1)}, u32[]{:S(2)}, u32[]{:S(2)}) collective-permute-start(bf16[1,128,128]{1,2,0:T(8,128)(2,1)S(1)} %bitcast.185), channel_id=1, source_target_pairs={{0,6},{2,8},{4,10},{6,12},{8,14},{10,16},{12,18},{14,20},{16,22},{... | collective-permute-start | bytes 98312 | tf_op jit(solution)/shard_map/ppermute | solution.py:17
  97.5 13.5 %collective-permute-start.17 = (f32[128,128]{0,1:T(8,128)S(1)}, f32[128,128]{0,1:T(8,128)S(1)}, u32[]{:S(2)}, u32[]{:S(2)}) collective-permute-start(f32[128,128]{0,1:T(8,128)S(1)} %convolution_bitcast_fusion.6), channel_id=1, source_target_pairs={{0,2},{2,0},{4,6},{6,4},{8,10},{10,8},{12,14},{14,12},{16,18},{18,... | collective-permute-start | bytes 196616 | tf_op jit(solution)/shard_map/ppermute | solution.py:11
  100.9 6.5 %collective-permute-start.25 = (f32[128,128]{0,1:T(8,128)S(1)}, f32[128,128]{0,1:T(8,128)S(1)}, u32[]{:S(2)}, u32[]{:S(2)}) collective-permute-start(f32[128,128]{0,1:T(8,128)S(1)} %add.107), channel_id=1, source_target_pairs={{0,4},{2,6},{4,0},{6,2},{8,12},{10,14},{12,8},{14,10},{16,20},{18,... | collective-permute-start | bytes 196616 | tf_op jit(solution)/shard_map/ppermute | solution.py:11
  107.5 8.3 %collective-permute-start.26 = (f32[64,128]{0,1:T(8,128)S(1)}, f32[64,128]{0,1:T(8,128)S(1)}, u32[]{:S(2)}, u32[]{:S(2)}) collective-permute-start(f32[64,128]{0,1:T(8,128)S(1)} %convolution_bitcast_fusion.3), channel_id=1, source_target_pairs={{0,2},{2,0},{4,6},{6,4},{8,10},{10,8},{12,14},{14,12},{16,18},{18,... | collective-permute-start | bytes 98312 | tf_op jit(solution)/shard_map/ppermute | solution.py:11
  (25 other events, 363.1 us)
Sparse Core Ops, SparseCore 0:
  106.9 44.6 all-gather.1
where the time goes:
time: 190 us; the launch traced here: 189 us
  starting transfers between devices  90.3 us (48%)
  waiting for transfers between devices  40.6 us (21%)
  local copies, waits for them, and re-layouts  20 us (11%)
  between operations  14.4 us (8%)
  matrix products  13.9 us (7%)
  other arithmetic  5.42 us (3%)
  blocking collectives  4.12 us (2%)
    ppermute x18, starting transfers between devices, from_behind(): return lax.ppermute(value, axis, pairs)  59.3 us
    all_gather x1, waiting for transfers between devices, body(): vec_window = lax.all_gather(window_vec, 'vec', axis=0, tiled=True)  30.3 us
    ppermute x7, starting transfers between devices, swapped(): lax.ppermute(value, axis, [(i, i ^ 1 << distance) for i in range(lax.axis...  27.7 us
    ppermute x7, waiting for transfers between devices, swapped(): lax.ppermute(value, axis, [(i, i ^ 1 << distance) for i in range(lax.axis...  9.5 us
    dot_general x2, matrix products, body(): jnp.einsum('vmq,mpq->vp', picked, tiles, preferred_element_type=jnp.float32)  8.42 us
    all_gather x1, local copies, waits for them, and re-layouts, body(): vec_window = lax.all_gather(window_vec, 'vec', axis=0, tiled=True)  4.43 us
    all_to_all x1, blocking collectives, body(): lax.all_to_all(near_mixed.astype(jnp.bfloat16), 'vec', split_axis=0, conc...  4.12 us
    gather x2, local copies, waits for them, and re-layouts, body(): picked = jnp.take(vec_grid, slot_pos, axis=1)  3.9 us
  transfers between devices with their start and end apart: 28, of which 8 were waited for; matrix products, arithmetic and copies ran while one was open for 6% of the time, Pallas kernels for 0%

commit v1 on v0

v1 whole, which is shorter than its diff:
```python
import functools
import math

import jax
import jax.numpy as jnp
from jax import lax
from jax.experimental import pallas as pl
from jax.experimental.pallas import tpu as pltpu
from jax.sharding import PartitionSpec as P

MESH = pl.DeviceIdType.MESH
bf16 = jnp.bfloat16
f32 = jnp.float32
SCALE = 80.0 * math.log2(math.e)
NT = (((1,), (1,)), ((), ()))


def nn(a, b):
    return jnp.dot(a, b, preferred_element_type=f32)


def nt(a, b):
    return lax.dot_general(a, b, NT, preferred_element_type=f32)


def split3(value):
    high = value.astype(bf16).astype(f32)
    rest = value - high
    middle = rest.astype(bf16).astype(f32)
    low = (rest - middle).astype(bf16).astype(f32)
    return high, middle, low


def stack_rows(rows, count):
    width = rows[0].shape[1]
    place = lax.broadcasted_iota(jnp.int32, (count, width), 0)
    out = jnp.zeros((count, width), f32)
    for r, row in enumerate(rows):
        out = jnp.where(place == r, jnp.broadcast_to(row, (count, width)), out)
    return out


class Links:
    def __init__(self, send_sem, recv_sem, core):
        self.send_sem, self.recv_sem, self.core = send_sem, recv_sem, core
        self.count = 0
        self.sent = []

    def new(self, src, dst, target, can_send, can_recv):
        slot = self.count
        self.count += 1
        copy = pltpu.make_async_remote_copy(
            src_ref=src,
            dst_ref=dst,
            send_sem=self.send_sem.at[slot],
            recv_sem=self.recv_sem.at[slot],
            device_id=(target, self.core),
            device_id_type=MESH,
        )
        self.sent.append((copy, can_send))
        return copy, can_send, can_recv

    @staticmethod
    def start(message):
        copy, can_send, _ = message
        if can_send is True:
            copy.start()
        else:
            pl.when(can_send)(copy.start)

    @staticmethod
    def arrive(message):
        copy, _, can_recv = message
        if can_recv is True:
            copy.wait_recv()
        else:
            pl.when(can_recv)(copy.wait_recv)

    def drain(self):
        for copy, can_send in self.sent:
            if can_send is True:
                copy.wait_send()
            else:
                pl.when(can_send)(copy.wait_send)


def kernel(
    size,
    vec_hbm, pts_hbm, basis_hbm, near_ref, e0_hbm, e1_hbm, e2_hbm, e3_hbm,
    c0_hbm, c1_hbm, c2_hbm, c3_hbm, c4_hbm,
    out_hbm,
    vec_in, pts, basis, e0, e1, e2, e3, c0, c1, c2, c3, c4,
    vw, gw, fw, l0, l1, l2own, l2, p3s, p3r, p4s, p4r, l3s, l3r, l4s, l4r,
    f3s, f3r, f4s, f4r, far0, near,
    load_sem, send_sem, recv_sem, out_sem,
):
    i = lax.axis_index("leaf")
    core = lax.axis_index("vec")
    half = i % 2
    y = i % 4
    pair = i + 1 - 2 * half
    line = (pair, i + 2 - 4 * ((i // 2) % 2), i + 3 - 2 * y)
    step4 = 4 * (y - 3 + 3 * (y // 2))

    def inside(d):
        return (d >= 0) & (d < size)

    three_to = (i + 6 - 10 * half, i + 4 - 10 * half)
    three_from = (i - 6 + 10 * half, i - 4 + 10 * half)
    barrier = pltpu.get_barrier_semaphore()

    def greet(target):
        pl.semaphore_signal(barrier, inc=1, device_id=(target, core), device_id_type=MESH)

    wanted = jnp.int32(0)
    for move in (-3, -2, -1, 1, 2, 3):
        pl.when(inside(i + move))(functools.partial(greet, i + move))
        wanted = wanted + inside(i + move).astype(jnp.int32)
    for source, target in zip(
        (*three_from, i + step4), (*three_to, i - step4), strict=True
    ):
        pl.when(inside(source))(functools.partial(greet, source))
        wanted = wanted + inside(target).astype(jnp.int32)

    loads = []

    def load(src, dst):
        copy = pltpu.make_async_copy(src, dst, load_sem.at[len(loads)])
        copy.start()
        loads.append(copy)
        return copy

    load_pts = load(pts_hbm, pts)
    load_vec = [
        load(vec_hbm.at[:, pl.ds(512 * l, 512)], vec_in.at[l]) for l in range(4)
    ]
    load_basis = [
        load(basis_hbm.at[pl.ds(512 * l, 512)], basis.at[l]) for l in range(4)
    ]
    load_e0 = load(e0_hbm, e0)
    load_e1 = load(e1_hbm, e1)
    load_e2 = load(e2_hbm, e2)
    load_e3 = load(e3_hbm, e3.at[pl.ds(pl.multiple_of(64 * half, 64), 64)])
    load_c = [
        load(s, d)
        for s, d in ((c4_hbm, c4), (c3_hbm, c3), (c2_hbm, c2), (c1_hbm, c1), (c0_hbm, c0))
    ]

    gw[:, 16:, :] = jnp.zeros((10, 112, 512), bf16)
    load_pts.wait()
    for l in range(4):
        x = pts[:, 512 * l : 512 * (l + 1)].astype(f32)
        rows = [x[k : k + 1] for k in range(3)]
        scaled = split3(x * SCALE)
        square = rows[0] * rows[0] + rows[1] * rows[1] + rows[2] * rows[2]
        squares = list(split3(square * (-0.5 * SCALE)))
        one = jnp.ones_like(square)
        cols = [s[k : k + 1] for s in scaled for k in range(3)]
        gw[3 + l, 0:16, :] = stack_rows(cols + [one] * 3 + squares, 16).astype(bf16)
        target_rows = stack_rows(rows * 3 + squares + [one] * 3, 16)
        padded = jnp.concatenate([target_rows, jnp.zeros((112, 512), f32)], axis=0)
        fw[l] = jnp.transpose(padded).astype(bf16)

    for l in range(4):
        load_vec[l].wait()
        vw[3 + l] = vec_in[l].astype(bf16)
    for l in range(4):
        load_basis[l].wait()
        l0[3 + l] = nn(vw[3 + l], basis[l]).astype(bf16)
    load_e0.wait()
    for t in range(2):
        l1[3 + t] = (nn(l0[3 + 2 * t], e0[2 * t]) + nn(l0[4 + 2 * t], e0[2 * t + 1])).astype(bf16)
    load_e1.wait()
    l2own[...] = (nn(l1[3], e1[0]) + nn(l1[4], e1[1])).astype(bf16)
    load_e2.wait()
    share3 = nn(l2own[...], e2[...])
    p3s[...] = share3.astype(bf16)

    def clear(ref):
        ref[...] = jnp.zeros(ref.shape, ref.dtype)

    def clear_all(*refs):
        for ref in refs:
            clear(ref)

    pl.when(i < 1)(lambda: clear_all(vw.at[0:3], gw.at[0:3, 0:16], l0.at[0:3], l1.at[1:3]))
    pl.when(i < 2)(lambda: clear_all(l1.at[0:1], l2.at[1]))
    pl.when(i < 3)(lambda: clear_all(l2.at[0]))
    pl.when(i > size - 2)(lambda: clear_all(vw.at[7:10], gw.at[7:10, 0:16], l0.at[7:10], l1.at[5:7]))
    pl.when(i > size - 3)(lambda: clear_all(l1.at[7:8], l2.at[2]))
    pl.when(i > size - 4)(lambda: clear_all(l2.at[3]))
    for k in range(2):
        pl.when(jnp.logical_not(inside(three_from[k])))(functools.partial(clear, l3r.at[k]))
    pl.when(jnp.logical_not(inside(i + step4)))(functools.partial(clear, l4r))

    links = Links(send_sem, recv_sem, core)

    def shift(src, dst, move):
        return links.new(src, dst, i + move, inside(i + move), inside(i - move))

    e3_rows = e3.at[pl.ds(pl.multiple_of(64 * half, 64), 64)]
    m_e3 = links.new(e3_rows, e3_rows, pair, True, True)
    m_p3 = links.new(p3s, p3r, pair, True, True)
    m_vec = []
    m_pts = []
    for k in range(3):
        m_vec.append(
            (shift(vw.at[6 - k], vw.at[2 - k], 1), shift(vw.at[3 + k], vw.at[7 + k], -1))
        )
        m_pts.append(
            (
                shift(gw.at[6 - k, pl.ds(0, 16)], gw.at[2 - k, pl.ds(0, 16)], 1),
                shift(gw.at[3 + k, pl.ds(0, 16)], gw.at[7 + k, pl.ds(0, 16)], -1),
            )
        )
    m_l0 = (
        shift(l0.at[pl.ds(4, 3)], l0.at[pl.ds(0, 3)], 1),
        shift(l0.at[pl.ds(3, 3)], l0.at[pl.ds(7, 3)], -1),
    )
    m_l1 = (
        shift(l1.at[pl.ds(3, 2)], l1.at[pl.ds(1, 2)], 1),
        shift(l1.at[pl.ds(3, 2)], l1.at[pl.ds(5, 2)], -1),
        shift(l1.at[4], l1.at[0], 2),
        shift(l1.at[3], l1.at[7], -2),
    )
    m_l2 = (
        shift(l2own, l2.at[0], 3),
        shift(l2own, l2.at[1], 2),
        shift(l2own, l2.at[2], -2),
        shift(l2own, l2.at[3], -3),
    )
    m_p4 = [links.new(p4s, p4r.at[k], line[k], True, True) for k in range(3)]
    m_l3 = [
        links.new(l3s, l3r.at[k], three_to[k], inside(three_to[k]), inside(three_from[k]))
        for k in range(2)
    ]
    m_l4 = links.new(l4s, l4r, i - step4, inside(i - step4), inside(i + step4))
    m_f3 = links.new(f3s, f3r, pair, True, True)
    m_f4 = [links.new(f4s, f4r.at[k], line[k], True, True) for k in range(3)]

    load_e3.wait()
    pl.semaphore_wait(barrier, wanted)

    for m in (m_e3, m_p3, *m_pts[0], *m_vec[0], *m_l2, *m_l1):
        links.start(m)
    for m in (*m_pts[1], *m_vec[1], *m_pts[2], *m_vec[2], *m_l0):
        links.start(m)

    def live(l, w):
        leaf = i * 4 + w - 3
        found = jnp.float32(0.0)
        for m in range(7):
            found = jnp.where(near_ref[l, m] == leaf, jnp.float32(1.0), found)
        return jnp.where(leaf >= 0, found, jnp.float32(0.0))

    def tile(l, w):
        block = jnp.exp2(nn(fw[l], gw[w])).astype(bf16)
        picked = vw[w] * live(l, w).astype(bf16)
        return nt(picked, block)

    def own_leaf(l, carry):
        total = tile(l, 3)
        for w in range(4, 7):
            total = total + tile(l, w)
        near[l] = total
        return carry

    lax.fori_loop(0, 1, own_leaf, 0)

    links.arrive(m_e3)
    links.arrive(m_p3)
    l3s[...] = (share3 + p3r[...].astype(f32)).astype(bf16)
    share4 = nn(p3s[...], e3[...])
    p4s[...] = share4.astype(bf16)
    for m in (*m_p4, *m_l3):
        links.start(m)

    lax.fori_loop(1, 2, own_leaf, 0)

    total4 = share4
    for k in range(3):
        links.arrive(m_p4[k])
        total4 = total4 + p4r[k].astype(f32)
    l4s[...] = total4.astype(bf16)
    links.start(m_l4)

    lax.fori_loop(2, 3, own_leaf, 0)

    for copy in load_c:
        copy.wait()
    for m in m_l3:
        links.arrive(m)
    far3 = nt(l3r[0], c3[0]) + nt(l3r[1], c3[1])
    f3s[...] = far3.astype(bf16)
    links.start(m_f3)
    links.arrive(m_l4)
    far4 = nt(l4r[...], c4[0])
    f4s[...] = far4.astype(bf16)
    for m in m_f4:
        links.start(m)

    lax.fori_loop(3, 4, own_leaf, 0)

    for m in (*m_pts[0], *m_vec[0]):
        links.arrive(m)

    def beside(l, carry):
        near[l] = near[l] + tile(l, 2)
        near[l + 1] = near[l + 1] + tile(l + 1, 7)
        return carry

    lax.fori_loop(0, 3, beside, 0)

    for m in (*m_l1, *m_l2):
        links.arrive(m)
    links.arrive(m_f3)
    for m in m_f4:
        links.arrive(m)
    down4 = far4
    for k in range(3):
        down4 = down4 + f4r[k].astype(f32)
    down3 = far3 + f3r[...].astype(f32) + nt(down4.astype(bf16), e3[...])
    far2 = nt(l2[0], c2[0]) + nt(l2[1], c2[1]) + nt(l2[2], c2[2]) + nt(l2[3], c2[3])
    down2 = (far2 + nt(down3.astype(bf16), e2[...])).astype(bf16)
    down1 = []
    for t in range(2):
        far1 = nt(l1[t], c1[4 * t]) + nt(l1[1 + t], c1[4 * t + 1])
        far1 = far1 + nt(l1[5 + t], c1[4 * t + 2]) + nt(l1[6 + t], c1[4 * t + 3])
        down1.append((far1 + nt(down2, e1[t])).astype(bf16))
    for l in range(4):
        far0[l] = nt(down1[l // 2], e0[l])

    for m in (*m_pts[1], *m_vec[1]):
        links.arrive(m)

    def second(l, carry):
        near[l] = near[l] + tile(l, 1)
        near[l + 2] = near[l + 2] + tile(l + 2, 8)
        return carry

    lax.fori_loop(0, 2, second, 0)

    for m in (*m_pts[2], *m_vec[2]):
        links.arrive(m)
    near[0] = near[0] + tile(0, 0)
    near[3] = near[3] + tile(3, 9)

    for m in m_l0:
        links.arrive(m)
    outs = []
    for l in range(4):
        far = far0[l] + nt(l0[l], c0[4 * l]) + nt(l0[l + 1], c0[4 * l + 1])
        far = far + nt(l0[l + 5], c0[4 * l + 2]) + nt(l0[l + 6], c0[4 * l + 3])
        near[l] = near[l] + nt(far.astype(bf16), basis[l])
        copy = pltpu.make_async_copy(
            near.at[l], out_hbm.at[:, pl.ds(512 * l, 512)], out_sem.at[l]
        )
        copy.start()
        outs.append(copy)
    links.drain()
    for copy in outs:
        copy.wait()


def body(size, vectors, points, basis, near_list, e0, e1, e2, e3, c0, c1, c2, c3, c4):
    vecs, count = vectors.shape
    rank = basis.shape[1]
    anywhere = pl.BlockSpec(memory_space=pl.ANY)
    return pl.pallas_call(
        functools.partial(kernel, size),
        out_shape=jax.ShapeDtypeStruct((vecs, count), f32),
        in_specs=[anywhere] * 3
        + [pl.BlockSpec(memory_space=pltpu.SMEM)]
        + [anywhere] * 9,
        out_specs=anywhere,
        scratch_shapes=[
            pltpu.VMEM((4, 128, 512), f32),
            pltpu.VMEM((3, 2048), bf16),
            pltpu.VMEM((4, 512, 128), bf16),
            pltpu.VMEM((4, 128, 128), bf16),
            pltpu.VMEM((2, 128, 128), bf16),
            pltpu.VMEM((128, 128), bf16),
            pltpu.VMEM((128, 128), bf16),
            pltpu.VMEM((16, 128, 128), bf16),
            pltpu.VMEM((8, 128, 128), bf16),
            pltpu.VMEM((4, 128, 128), bf16),
            pltpu.VMEM((2, 128, 128), bf16),
            pltpu.VMEM((1, 128, 128), bf16),
            pltpu.VMEM((10, 128, 512), bf16),
            pltpu.VMEM((10, 128, 512), bf16),
            pltpu.VMEM((4, 512, 128), bf16),
            pltpu.VMEM((10, 128, 128), bf16),
            pltpu.VMEM((8, 128, 128), bf16),
            pltpu.VMEM((128, 128), bf16),
            pltpu.VMEM((4, 128, 128), bf16),
            pltpu.VMEM((128, 128), bf16),
            pltpu.VMEM((128, 128), bf16),
            pltpu.VMEM((128, 128), bf16),
            pltpu.VMEM((3, 128, 128), bf16),
            pltpu.VMEM((128, 128), bf16),
            pltpu.VMEM((2, 128, 128), bf16),
            pltpu.VMEM((128, 128), bf16),
            pltpu.VMEM((128, 128), bf16),
            pltpu.VMEM((128, 128), bf16),
            pltpu.VMEM((128, 128), bf16),
            pltpu.VMEM((128, 128), bf16),
            pltpu.VMEM((3, 128, 128), bf16),
            pltpu.VMEM((4, 128, 128), f32),
            pltpu.VMEM((4, 128, 512), f32),
            pltpu.SemaphoreType.DMA((24,)),
            pltpu.SemaphoreType.DMA((40,)),
            pltpu.SemaphoreType.DMA((40,)),
            pltpu.SemaphoreType.DMA((4,)),
        ],
        compiler_params=pltpu.CompilerParams(
            collective_id=0, has_side_effects=True, vmem_limit_bytes=48 * 2**20
        ),
        cost_estimate=pl.CostEstimate(
            flops=6_000_000_000, bytes_accessed=4_000_000, transcendentals=7_340_032
        ),
    )(
        vectors, points, basis, near_list,
        e0.reshape(-1, rank, rank), e1.reshape(-1, rank, rank), e2, e3,
        c0, c1, c2, c3, c4,
    )


def solution(mesh):
    placed = (
        P("vec", "leaf"),
        P(None, "leaf"),
        *[P("leaf", None)] * 6,
        *[P("leaf", None, None)] * 5,
    )
    return jax.shard_map(
        functools.partial(body, mesh.shape["leaf"]),
        mesh=mesh,
        in_specs=placed,
        out_specs=P("vec", "leaf"),
        check_vma=False,
    )
```

time: 190 us -> 57.1 us (0.30)
  the two profiles are of different devices: /device:TPU:1 before, /device:TPU:392 now
where the time goes in v1:
time: 57.1 us; the launch traced here: 56.4 us
  Pallas kernels  44 us (77%)
  local copies, waits for them, and re-layouts  12.3 us (22%)
    pallas_call x1, Pallas kernels, body(): pl.pallas_call(functools.partial(kernel, size), out_shape=jax.ShapeDtypeS...  44 us
    unnamed x27, local copies, waits for them, and re-layouts  12.3 us

profile of v1, /device:TPU:392, one launch (start us, length us, event | category | flops | bytes accessed | tf_op | source)
XLA Modules:
  0.0 56.4 jit_solution(1105877106740296363)
XLA Ops:
  0.0 0.0 copy-start.12
  0.0 0.7 %copy-done.12 = s32[4,7]{1,0:T(4,128)S(1)} copy-done((s32[4,7]{1,0:T(4,128)S(1)}, s32[4,7]{1,0:T(4,128)}, u32[]{:S(2)}) %copy-start.12) | copy-done | bytes 136
  0.7 0.0 copy-start
  0.7 1.2 %copy-done = f32[128,2048]{1,0:T(8,128)S(1)} copy-done((f32[128,2048]{1,0:T(8,128)S(1)}, f32[128,2048]{1,0:T(8,128)}, u32[]{:S(2)}) %copy-start) | copy-done | bytes 1048600
  1.9 0.0 copy-start.1
  1.9 1.0 %copy-done.1 = bf16[2048,128]{1,0:T(8,128)(2,1)S(1)} copy-done((bf16[2048,128]{1,0:T(8,128)(2,1)S(1)}, bf16[2048,128]{1,0:T(8,128)(2,1)}, u32[]{:S(2)}) %copy-start.1) | copy-done | bytes 524312
  3.0 0.0 copy-start.2
  3.0 1.0 %copy-done.2 = bf16[16,128,128]{2,1,0:T(8,128)(2,1)S(1)} copy-done((bf16[16,128,128]{2,1,0:T(8,128)(2,1)S(1)}, bf16[16,128,128]{2,1,0:T(8,128)(2,1)}, u32[]{:S(2)}) %copy-start.2) | copy-done | bytes 524312
  4.0 0.0 copy-start.3
  4.0 0.9 %copy-done.3 = bf16[8,128,128]{2,1,0:T(8,128)(2,1)S(1)} copy-done((bf16[8,128,128]{2,1,0:T(8,128)(2,1)S(1)}, bf16[8,128,128]{2,1,0:T(8,128)(2,1)}, u32[]{:S(2)}) %copy-start.3) | copy-done | bytes 262168
  4.9 0.0 copy-start.4
  4.9 0.9 %copy-done.4 = bf16[512,128]{1,0:T(8,128)(2,1)S(1)} copy-done((bf16[512,128]{1,0:T(8,128)(2,1)S(1)}, bf16[512,128]{1,0:T(8,128)(2,1)}, u32[]{:S(2)}) %copy-start.4) | copy-done | bytes 131096
  5.8 0.0 copy-start.5
  5.8 0.9 %copy-done.5 = bf16[4,128,128]{2,1,0:T(8,128)(2,1)S(1)} copy-done((bf16[4,128,128]{2,1,0:T(8,128)(2,1)S(1)}, bf16[4,128,128]{2,1,0:T(8,128)(2,1)}, u32[]{:S(2)}) %copy-start.5) | copy-done | bytes 131096
  6.8 0.0 copy-start.6
  6.8 0.8 %copy-done.6 = bf16[256,128]{1,0:T(8,128)(2,1)S(1)} copy-done((bf16[256,128]{1,0:T(8,128)(2,1)S(1)}, bf16[256,128]{1,0:T(8,128)(2,1)}, u32[]{:S(2)}) %copy-start.6) | copy-done | bytes 65560
  7.6 0.0 copy-start.7
  7.6 0.8 %copy-done.7 = bf16[2,128,128]{2,1,0:T(8,128)(2,1)S(1)} copy-done((bf16[2,128,128]{2,1,0:T(8,128)(2,1)S(1)}, bf16[2,128,128]{2,1,0:T(8,128)(2,1)}, u32[]{:S(2)}) %copy-start.7) | copy-done | bytes 65560
  8.4 0.8 %copy-done.8 = bf16[128,128]{1,0:T(8,128)(2,1)S(1)} copy-done((bf16[128,128]{1,0:T(8,128)(2,1)S(1)}, bf16[128,128]{1,0:T(8,128)(2,1)}, u32[]{:S(2)}) %copy-start.8) | copy-done | bytes 32792
  9.2 0.8 %copy-done.9 = bf16[1,128,128]{2,1,0:T(8,128)(2,1)S(1)} copy-done((bf16[1,128,128]{2,1,0:T(8,128)(2,1)S(1)}, bf16[1,128,128]{2,1,0:T(8,128)(2,1)}, u32[]{:S(2)}) %copy-start.9) | copy-done | bytes 32792
  10.0 0.7 %copy-done.10 = bf16[3,2048]{1,0:T(4,128)(2,1)S(1)} copy-done((bf16[3,2048]{1,0:T(4,128)(2,1)S(1)}, bf16[3,2048]{1,0:T(4,128)(2,1)}, u32[]{:S(2)}) %copy-start.10) | copy-done | bytes 12312
  10.7 0.7 %copy-done.11 = bf16[64,128]{1,0:T(8,128)(2,1)S(1)} copy-done((bf16[64,128]{1,0:T(8,128)(2,1)S(1)}, bf16[64,128]{1,0:T(8,128)(2,1)}, u32[]{:S(2)}) %copy-start.11) | copy-done | bytes 16408
  11.4 44.0 %shard_map.127 = f32[128,2048]{1,0:T(8,128)S(1)} custom-call(f32[128,2048]{1,0:T(8,128)S(1)} %copy-done, bf16[3,2048]{1,0:T(4,128)(2,1)S(1)} %copy-done.10, bf16[2048,128]{1,0:T(8,128)(2,1)S(1)} %copy-done.1, s32[4,7]{1,0:T(4,128)S(1)} %copy-done.12, bf16[4,128,128]{2,1,0:T(8,128)(2,1)S(1)} %bitcast.2, bf16[2,128,128]{2,1,0:T(8,128)(2,1)S(1)} %bitcast.3, ...), custom_call_target="tpu_custom_call" | custom-call | flops 6000000000 | bytes 4000000 | tf_op jit(solution)/shard_map/pallas_call | solution.py:369
  55.4 1.0 %copy.15 = f32[128,2048]{1,0:T(8,128)} copy(f32[128,2048]{1,0:T(8,128)S(1)} %shard_map.127) | data formatting | bytes 2097152
  (4 shorter events, 0.0 us)
Async XLA Ops:
  0.0 0.7 %copy-start.12 = (s32[4,7]{1,0:T(4,128)S(1)}, s32[4,7]{1,0:T(4,128)}, u32[]{:S(2)}) copy-start(s32[4,7]{1,0:T(4,128)} %near_ref.1) | copy-start | bytes 340
  0.7 1.2 %copy-start = (f32[128,2048]{1,0:T(8,128)S(1)}, f32[128,2048]{1,0:T(8,128)}, u32[]{:S(2)}) copy-start(f32[128,2048]{1,0:T(8,128)} %vec_hbm.1) | copy-start | bytes 3145732
  1.9 1.0 %copy-start.1 = (bf16[2048,128]{1,0:T(8,128)(2,1)S(1)}, bf16[2048,128]{1,0:T(8,128)(2,1)}, u32[]{:S(2)}) copy-start(bf16[2048,128]{1,0:T(8,128)(2,1)} %basis_hbm.1) | copy-start | bytes 1572868
  3.0 1.0 %copy-start.2 = (bf16[16,128,128]{2,1,0:T(8,128)(2,1)S(1)}, bf16[16,128,128]{2,1,0:T(8,128)(2,1)}, u32[]{:S(2)}) copy-start(bf16[16,128,128]{2,1,0:T(8,128)(2,1)} %c0_hbm.1) | copy-start | bytes 1572868
  4.0 0.9 %copy-start.3 = (bf16[8,128,128]{2,1,0:T(8,128)(2,1)S(1)}, bf16[8,128,128]{2,1,0:T(8,128)(2,1)}, u32[]{:S(2)}) copy-start(bf16[8,128,128]{2,1,0:T(8,128)(2,1)} %c1_hbm.1) | copy-start | bytes 786436
  4.9 0.9 %copy-start.4 = (bf16[512,128]{1,0:T(8,128)(2,1)S(1)}, bf16[512,128]{1,0:T(8,128)(2,1)}, u32[]{:S(2)}) copy-start(bf16[512,128]{1,0:T(8,128)(2,1)} %param.17) | copy-start | bytes 393220
  5.8 0.9 %copy-start.5 = (bf16[4,128,128]{2,1,0:T(8,128)(2,1)S(1)}, bf16[4,128,128]{2,1,0:T(8,128)(2,1)}, u32[]{:S(2)}) copy-start(bf16[4,128,128]{2,1,0:T(8,128)(2,1)} %c2_hbm.1) | copy-start | bytes 393220
  6.8 0.8 %copy-start.6 = (bf16[256,128]{1,0:T(8,128)(2,1)S(1)}, bf16[256,128]{1,0:T(8,128)(2,1)}, u32[]{:S(2)}) copy-start(bf16[256,128]{1,0:T(8,128)(2,1)} %param.18) | copy-start | bytes 196612
  7.6 0.8 %copy-start.7 = (bf16[2,128,128]{2,1,0:T(8,128)(2,1)S(1)}, bf16[2,128,128]{2,1,0:T(8,128)(2,1)}, u32[]{:S(2)}) copy-start(bf16[2,128,128]{2,1,0:T(8,128)(2,1)} %c3_hbm.1) | copy-start | bytes 196612
  8.4 0.8 %copy-start.8 = (bf16[128,128]{1,0:T(8,128)(2,1)S(1)}, bf16[128,128]{1,0:T(8,128)(2,1)}, u32[]{:S(2)}) copy-start(bf16[128,128]{1,0:T(8,128)(2,1)} %e2_hbm.1) | copy-start | bytes 98308
  9.2 0.8 %copy-start.9 = (bf16[1,128,128]{2,1,0:T(8,128)(2,1)S(1)}, bf16[1,128,128]{2,1,0:T(8,128)(2,1)}, u32[]{:S(2)}) copy-start(bf16[1,128,128]{2,1,0:T(8,128)(2,1)} %c4_hbm.1) | copy-start | bytes 98308
  9.9 0.7 %copy-start.10 = (bf16[3,2048]{1,0:T(4,128)(2,1)S(1)}, bf16[3,2048]{1,0:T(4,128)(2,1)}, u32[]{:S(2)}) copy-start(bf16[3,2048]{1,0:T(4,128)(2,1)} %pts_hbm.1) | copy-start | bytes 36868
  10.7 0.7 %copy-start.11 = (bf16[64,128]{1,0:T(8,128)(2,1)S(1)}, bf16[64,128]{1,0:T(8,128)(2,1)}, u32[]{:S(2)}) copy-start(bf16[64,128]{1,0:T(8,128)(2,1)} %e3_hbm.1) | copy-start | bytes 49156

commit v2 on v1

v2 whole, which is shorter than its diff:
```python
import functools
import math

import jax
import jax.numpy as jnp
from jax import lax
from jax.experimental import pallas as pl
from jax.experimental.pallas import tpu as pltpu
from jax.sharding import PartitionSpec as P

MESH = pl.DeviceIdType.MESH
bf16 = jnp.bfloat16
f32 = jnp.float32
SCALE = 80.0 * math.log2(math.e)
NT = (((1,), (1,)), ((), ()))
offsets = (-3, -2, 2, 3)


def nn(a, b):
    return jnp.dot(a, b, preferred_element_type=f32)


def nt(a, b):
    return lax.dot_general(a, b, NT, preferred_element_type=f32)


def split3(value):
    high = value.astype(bf16).astype(f32)
    rest = value - high
    middle = rest.astype(bf16).astype(f32)
    low = (rest - middle).astype(bf16).astype(f32)
    return high, middle, low


def stack_rows(rows, count):
    width = rows[0].shape[1]
    place = lax.broadcasted_iota(jnp.int32, (count, width), 0)
    out = jnp.zeros((count, width), f32)
    for r, row in enumerate(rows):
        out = jnp.where(place == r, jnp.broadcast_to(row, (count, width)), out)
    return out


class Links:
    def __init__(self, send_sem, recv_sem, core):
        self.send_sem, self.recv_sem, self.core = send_sem, recv_sem, core
        self.sends = self.recvs = 0
        self.sent = []

    def copy(self, src, dst, target, send_slot, recv_slot):
        return pltpu.make_async_remote_copy(
            src_ref=src,
            dst_ref=dst,
            send_sem=self.send_sem.at[send_slot],
            recv_sem=self.recv_sem.at[recv_slot],
            device_id=(target, self.core),
            device_id_type=MESH,
        )

    def out(self, src, dst, target, recv_slot, valid=True):
        copy = self.copy(src, dst, target, self.sends, recv_slot)
        self.sends += 1
        self.sent.append((copy, valid))
        when(valid, copy.start)

    def drain(self):
        for copy, valid in self.sent:
            when(valid, copy.wait_send)


def when(valid, act):
    if valid is True:
        act()
    else:
        pl.when(valid)(act)


def kernel(
    size,
    vec_hbm, pts_hbm, basis_hbm, near_hbm, e0_hbm, e1_hbm, e2_hbm, e3_hbm,
    c0_hbm, c1_hbm, c2_hbm, c3_hbm, c4_hbm,
    out,
    vec_in, pts, basis, near_ref, e0, e1, e2, e3, c0, c1, c2, c3, c4,
    vw, gw, fw, ptd, ptf, x3, l0, l1, l2own, l2, p3s, p4s, l3r, l4r,
    f3s, f3r, f4s, f4r, far0,
    load_sem, send_sem, recv_sem,
):
    i = lax.axis_index("leaf")
    core = lax.axis_index("vec")
    half = i % 2
    y = i % 4
    two, four = i // 2, i // 4
    pair = i + 1 - 2 * half
    line = (pair, i + 2 - 4 * ((i // 2) % 2), i + 3 - 2 * y)

    def inside(d):
        return (d >= 0) & (d < size)

    three_to = (2 * (two + 3), 2 * (two + 2), 2 * (two - 2) + 1, 2 * (two - 3) + 1)
    three_from = [2 * (two - 3 + 5 * half + slot) + k for slot in range(2) for k in range(2)]
    four_to = [4 * (four - offsets[j]) + j for j in range(4)]
    my_offset = y - 3 + 3 * (y // 2)
    four_from = [4 * (four + my_offset) + k for k in range(4)]

    barrier = pltpu.get_barrier_semaphore()

    def greet(target):
        pl.semaphore_signal(barrier, inc=1, device_id=(target, core), device_id_type=MESH)

    wanted = jnp.int32(0)
    near_by = [i + move for move in (-3, -2, -1, 1, 2, 3)]
    for source in (*near_by, *three_from, *four_from):
        pl.when(inside(source))(functools.partial(greet, source))
    for target in (*near_by, *three_to, *four_to):
        wanted = wanted + inside(target).astype(jnp.int32)

    loads = []

    def load(src, dst):
        copy = pltpu.make_async_copy(src, dst, load_sem.at[len(loads)])
        copy.start()
        loads.append(copy)
        return copy

    load_vec = [
        load(vec_hbm.at[:, pl.ds(512 * l, 512)], vec_in.at[l]) for l in (3, 0, 2, 1)
    ]
    load_pts = load(pts_hbm, pts)
    e3_rows = e3.at[pl.ds(pl.multiple_of(64 * half, 64), 64)]
    load_e3 = load(e3_hbm, e3_rows)
    load_basis = [
        load(basis_hbm.at[pl.ds(512 * l, 512)], basis.at[l]) for l in range(4)
    ]
    load_e = [load(s, d) for s, d in ((e0_hbm, e0), (e1_hbm, e1), (e2_hbm, e2))]
    load_near = load(near_hbm, near_ref)
    load_c = [
        load(s, d)
        for s, d in ((c4_hbm, c4), (c3_hbm, c3), (c2_hbm, c2), (c1_hbm, c1), (c0_hbm, c0))
    ]

    def clear_all(*refs):
        for ref in refs:
            ref[...] = jnp.zeros(ref.shape, ref.dtype)

    pl.when(i < 1)(lambda: clear_all(vw.at[0:3], ptd.at[0:3], l0.at[0:3], l1.at[1:3]))
    pl.when(i < 2)(lambda: clear_all(l1.at[0:1], l2.at[1]))
    pl.when(i < 3)(lambda: clear_all(l2.at[0]))
    pl.when(i > size - 2)(lambda: clear_all(vw.at[7:10], ptd.at[7:10], l0.at[7:10], l1.at[5:7]))
    pl.when(i > size - 3)(lambda: clear_all(l1.at[7:8], l2.at[2]))
    pl.when(i > size - 4)(lambda: clear_all(l2.at[3]))
    for k in range(4):
        pl.when(jnp.logical_not(inside(three_from[k])))(functools.partial(clear_all, l3r.at[k]))
        pl.when(jnp.logical_not(inside(four_from[k])))(functools.partial(clear_all, l4r.at[k]))

    load_pts.wait()
    place = lax.broadcasted_iota(jnp.int32, (16, 128), 0)
    for l in range(4):
        x = pts[:, 512 * l : 512 * (l + 1)].astype(f32)
        dense = jnp.zeros((16, 128), f32)
        for k in range(3):
            for b in range(4):
                piece = jnp.broadcast_to(x[k : k + 1, 128 * b : 128 * (b + 1)], (16, 128))
                dense = jnp.where(place == 4 * k + b, piece, dense)
        ptd[3 + l] = dense.astype(bf16)
    for copy, l in zip(load_vec, (3, 0, 2, 1), strict=True):
        copy.wait()
        vw[3 + l] = vec_in[l].astype(bf16)
    load_e3.wait()

    links = Links(send_sem, recv_sem, core)
    slots = iter(range(40))
    arrivals = {}

    def arrival(name, dst, valid=True):
        slot = next(slots)
        arrivals[name] = (links.copy(dst, dst, pair, 0, slot), valid)
        return slot

    def arrive(*names):
        for name in names:
            copy, valid = arrivals[name]
            when(valid, copy.wait_recv)

    def shift(name, src, dst, move):
        slot = arrival(name, dst, inside(i - move))
        links.out(src, dst, i + move, slot, inside(i + move))

    def vec_out(k):
        shift(("vec", k, 0), vw.at[6 - k], vw.at[2 - k], 1)
        shift(("vec", k, 1), vw.at[3 + k], vw.at[7 + k], -1)

    pl.semaphore_wait(barrier, wanted)

    other_rows = e3.at[pl.ds(pl.multiple_of(64 - 64 * half, 64), 64)]
    slot = arrival("e3", other_rows)
    links.out(e3_rows, e3_rows, pair, slot)
    shift(("pts", 0), ptd.at[pl.ds(4, 3)], ptd.at[pl.ds(0, 3)], 1)
    shift(("pts", 1), ptd.at[pl.ds(3, 3)], ptd.at[pl.ds(7, 3)], -1)
    vec_out(0)

    for l in range(4):
        load_basis[l].wait()
        l0[3 + l] = nn(vw[3 + l], basis[l]).astype(bf16)
    load_e[0].wait()
    for t in range(2):
        l1[3 + t] = (nn(l0[3 + 2 * t], e0[2 * t]) + nn(l0[4 + 2 * t], e0[2 * t + 1])).astype(bf16)
    load_e[1].wait()
    l2own[...] = (nn(l1[3], e1[0]) + nn(l1[4], e1[1])).astype(bf16)
    load_e[2].wait()
    p3s[...] = nn(l2own[...], e2[...]).astype(bf16)

    slot3 = [arrival(("p3", k), l3r.at[k], inside(three_from[k])) for k in range(4)]
    for j, target in enumerate(three_to):
        row = 2 * (j % 2) + half
        links.out(p3s, l3r.at[row], target, slot3[0] + row, inside(target))
    shift(("l2", 0), l2own, l2.at[0], 3)
    shift(("l2", 1), l2own, l2.at[1], 2)
    shift(("l2", 2), l2own, l2.at[2], -2)
    shift(("l2", 3), l2own, l2.at[3], -3)
    shift(("l1", 0), l1.at[pl.ds(3, 2)], l1.at[pl.ds(1, 2)], 1)
    shift(("l1", 1), l1.at[pl.ds(3, 2)], l1.at[pl.ds(5, 2)], -1)
    shift(("l1", 2), l1.at[4], l1.at[0], 2)
    shift(("l1", 3), l1.at[3], l1.at[7], -2)
    vec_out(1)

    def source_factors(w):
        rows = [x3[w, pl.ds(k, 1), :] for k in range(3)]
        square = rows[0] * rows[0] + rows[1] * rows[1] + rows[2] * rows[2]
        squares = list(split3(square * (-0.5 * SCALE)))
        one = jnp.ones_like(square)
        scaled = [split3(row * SCALE) for row in rows]
        cols = [scaled[k][part] for part in range(3) for k in range(3)]
        gw[w, 0:16, :] = stack_rows(cols + [one] * 3 + squares, 16).astype(bf16)
        return rows, squares, one

    def spread(w):
        ptf[w] = ptd[w].astype(f32)
        for k in range(3):
            for b in range(4):
                x3[w, pl.ds(k, 1), 128 * b : 128 * (b + 1)] = ptf[w, pl.ds(4 * k + b, 1), :]

    gw[:, 16:, :] = jnp.zeros((10, 112, 512), bf16)
    for l in range(4):
        spread(3 + l)
        rows, squares, one = source_factors(3 + l)
        target_rows = stack_rows(rows * 3 + squares + [one] * 3, 16)
        padded = jnp.concatenate([target_rows, jnp.zeros((112, 512), f32)], axis=0)
        fw[l] = jnp.transpose(padded).astype(bf16)

    arrive("e3")
    p4s[...] = nn(p3s[...], e3[...]).astype(bf16)
    slot4 = [arrival(("p4", k), l4r.at[k], inside(four_from[k])) for k in range(4)]
    for target in four_to:
        links.out(p4s, l4r.at[y], target, slot4[0] + y, inside(target))
    vec_out(2)
    shift(("l0", 0), l0.at[pl.ds(4, 3)], l0.at[pl.ds(0, 3)], 1)
    shift(("l0", 1), l0.at[pl.ds(3, 3)], l0.at[pl.ds(7, 3)], -1)
    load_near.wait()

    def live(l, w):
        leaf = i * 4 + w - 3
        found = jnp.float32(0.0)
        for m in range(7):
            found = jnp.where(near_ref[l, m] == leaf, jnp.float32(1.0), found)
        return jnp.where(leaf >= 0, found, jnp.float32(0.0))

    def tile(l, w):
        block = jnp.exp2(nn(fw[l], gw[w])).astype(bf16)
        picked = vw[w] * live(l, w).astype(bf16)
        return nt(picked, block)

    def columns(l):
        return pl.ds(pl.multiple_of(512 * l, 512), 512)

    def own_leaf(l, carry):
        total = tile(l, 3)
        for w in range(4, 7):
            total = total + tile(l, w)
        out[:, columns(l)] = total
        return carry

    lax.fori_loop(0, 2, own_leaf, 0)

    for copy in load_c:
        copy.wait()
    arrive(*[("p3", k) for k in range(4)])
    far3 = jnp.zeros((128, 128), f32)
    for k in range(2):
        low3 = (l3r[2 * k].astype(f32) + l3r[2 * k + 1].astype(f32)).astype(bf16)
        far3 = far3 + nt(low3, c3[k])
    f3s[...] = far3.astype(bf16)
    links.out(f3s, f3r, pair, arrival("f3", f3r))
    arrive(*[("p4", k) for k in range(4)])
    low4 = l4r[0].astype(f32)
    for k in range(1, 4):
        low4 = low4 + l4r[k].astype(f32)
    far4 = nt(low4.astype(bf16), c4[0])
    f4s[...] = far4.astype(bf16)
    for k in range(3):
        links.out(f4s, f4r.at[k], line[k], arrival(("f4", k), f4r.at[k]))

    lax.fori_loop(2, 4, own_leaf, 0)

    arrive(("pts", 0), ("pts", 1))
    for w in (2, 7, 1, 8, 0, 9):
        spread(w)
        source_factors(w)

    def add(l, value):
        out[:, columns(l)] = out[:, columns(l)] + value

    def beside(l, carry):
        add(l, tile(l, 2))
        add(l + 1, tile(l + 1, 7))
        return carry

    arrive(("vec", 0, 0), ("vec", 0, 1))
    lax.fori_loop(0, 3, beside, 0)

    arrive(*[("l2", k) for k in range(4)], *[("l1", k) for k in range(4)])
    far2 = nt(l2[0], c2[0]) + nt(l2[1], c2[1]) + nt(l2[2], c2[2]) + nt(l2[3], c2[3])
    far1 = []
    for t in range(2):
        part = nt(l1[t], c1[4 * t]) + nt(l1[1 + t], c1[4 * t + 1])
        far1.append(part + nt(l1[5 + t], c1[4 * t + 2]) + nt(l1[6 + t], c1[4 * t + 3]))
    arrive("f3", *[("f4", k) for k in range(3)])
    down4 = far4
    for k in range(3):
        down4 = down4 + f4r[k].astype(f32)
    down3 = far3 + f3r[...].astype(f32) + nt(down4.astype(bf16), e3[...])
    down2 = (far2 + nt(down3.astype(bf16), e2[...])).astype(bf16)
    down1 = [(far1[t] + nt(down2, e1[t])).astype(bf16) for t in range(2)]
    for l in range(4):
        far0[l] = nt(down1[l // 2], e0[l])

    def second(l, carry):
        add(l, tile(l, 1))
        add(l + 2, tile(l + 2, 8))
        return carry

    arrive(("vec", 1, 0), ("vec", 1, 1))
    lax.fori_loop(0, 2, second, 0)
    arrive(("vec", 2, 0), ("vec", 2, 1))
    add(0, tile(0, 0))
    add(3, tile(3, 9))

    arrive(("l0", 0), ("l0", 1))
    for l in range(4):
        far = far0[l] + nt(l0[l], c0[4 * l]) + nt(l0[l + 1], c0[4 * l + 1])
        far = far + nt(l0[l + 5], c0[4 * l + 2]) + nt(l0[l + 6], c0[4 * l + 3])
        add(l, nt(far.astype(bf16), basis[l]))
    links.drain()


def body(size, vectors, points, basis, near_list, e0, e1, e2, e3, c0, c1, c2, c3, c4):
    vecs, count = vectors.shape
    rank = basis.shape[1]
    hbm = pl.BlockSpec(memory_space=pltpu.HBM)
    square = pltpu.VMEM((rank, rank), bf16)

    def squares(count):
        return pltpu.VMEM((count, rank, rank), bf16)

    return pl.pallas_call(
        functools.partial(kernel, size),
        out_shape=jax.ShapeDtypeStruct((vecs, count), f32),
        in_specs=[hbm] * 13,
        out_specs=pl.BlockSpec(memory_space=pltpu.VMEM),
        scratch_shapes=[
            pltpu.VMEM((4, 128, 512), f32),
            pltpu.VMEM((3, 2048), bf16),
            pltpu.VMEM((4, 512, 128), bf16),
            pltpu.SMEM((4, 7), jnp.int32),
            squares(4),
            squares(2),
            square,
            square,
            squares(16),
            squares(8),
            squares(4),
            squares(2),
            squares(1),
            pltpu.VMEM((10, 128, 512), bf16),
            pltpu.VMEM((10, 128, 512), bf16),
            pltpu.VMEM((4, 512, 128), bf16),
            pltpu.VMEM((10, 16, 128), bf16),
            pltpu.VMEM((10, 16, 128), f32),
            pltpu.VMEM((10, 8, 512), f32),
            squares(10),
            squares(8),
            square,
            squares(4),
            square,
            square,
            squares(4),
            squares(4),
            square,
            square,
            square,
            squares(3),
            pltpu.VMEM((4, 128, 128), f32),
            pltpu.SemaphoreType.DMA((24,)),
            pltpu.SemaphoreType.DMA((40,)),
            pltpu.SemaphoreType.DMA((40,)),
        ],
        compiler_params=pltpu.CompilerParams(
            collective_id=0, has_side_effects=True, vmem_limit_bytes=60 * 2**20
        ),
        cost_estimate=pl.CostEstimate(
            flops=6_000_000_000, bytes_accessed=4_000_000, transcendentals=7_340_032
        ),
    )(
        vectors, points, basis, near_list,
        e0.reshape(-1, rank, rank), e1.reshape(-1, rank, rank), e2, e3,
        c0, c1, c2, c3, c4,
    )


def solution(mesh):
    placed = (
        P("vec", "leaf"),
        P(None, "leaf"),
        *[P("leaf", None)] * 6,
        *[P("leaf", None, None)] * 5,
    )
    return jax.shard_map(
        functools.partial(body, mesh.shape["leaf"]),
        mesh=mesh,
        in_specs=placed,
        out_specs=P("vec", "leaf"),
        check_vma=False,
    )
```

time: 57.1 us -> 40.6 us (0.71)
  the two profiles are of different devices: /device:TPU:392 before, /device:TPU:384 now
where the time goes in v2:
time: 40.6 us; the launch traced here: 40.5 us
  Pallas kernels  38.1 us (94%)
  local copies, waits for them, and re-layouts  2.3 us (6%)
    pallas_call x1, Pallas kernels, body(): pl.pallas_call(functools.partial(kernel, size), out_shape=jax.ShapeDtypeS...  38.1 us
    unnamed x1, local copies, waits for them, and re-layouts  2.3 us

profile of v2, /device:TPU:384, one launch (start us, length us, event | category | flops | bytes accessed | tf_op | source)
XLA Modules:
  0.0 40.5 jit_solution(16381387882367724308)
XLA Ops:
  0.0 38.1 %shard_map.127 = f32[128,2048]{1,0:T(8,128)} custom-call(f32[128,2048]{1,0:T(8,128)} %vec_hbm.1, bf16[3,2048]{1,0:T(4,128)(2,1)} %pts_hbm.1, bf16[2048,128]{1,0:T(8,128)(2,1)} %basis_hbm.1, s32[4,7]{1,0:T(4,128)} %near_hbm.1, bf16[4,128,128]{2,1,0:T(8,128)(2,1)} %bitcast.2, bf16[2,128,128]{2,1,0:T(8,128)(2,1)} %bitcast.3, bf16[128,128]{1,0:T(8,128)(2,1)} %e2_hbm.1, ...), custom_call_target="tpu_custom_call" | custom-call | flops 6000000000 | bytes 4000000 | tf_op jit(solution)/shard_map/pallas_call | solution.py:364
  38.2 2.3 %copy.15 = f32[128,2048]{1,0:T(8,128)} copy(f32[128,2048]{1,0:T(8,128)} %shard_map.127) | data formatting | bytes 2097152

commit v3 on v2

--- a/solution.py
+++ b/solution.py
@@ -14,6 +14,7 @@
 SCALE = 80.0 * math.log2(math.e)
 NT = (((1,), (1,)), ((), ()))
 offsets = (-3, -2, 2, 3)
+COPIES = 8
 
 
 def nn(a, b):
@@ -221,7 +222,6 @@
     shift(("l1", 1), l1.at[pl.ds(3, 2)], l1.at[pl.ds(5, 2)], -1)
     shift(("l1", 2), l1.at[4], l1.at[0], 2)
     shift(("l1", 3), l1.at[3], l1.at[7], -2)
-    vec_out(1)
 
     def source_factors(w):
         rows = [x3[w, pl.ds(k, 1), :] for k in range(3)]
@@ -252,9 +252,6 @@
     slot4 = [arrival(("p4", k), l4r.at[k], inside(four_from[k])) for k in range(4)]
     for target in four_to:
         links.out(p4s, l4r.at[y], target, slot4[0] + y, inside(target))
-    vec_out(2)
-    shift(("l0", 0), l0.at[pl.ds(4, 3)], l0.at[pl.ds(0, 3)], 1)
-    shift(("l0", 1), l0.at[pl.ds(3, 3)], l0.at[pl.ds(7, 3)], -1)
     load_near.wait()
 
     def live(l, w):
@@ -279,7 +276,16 @@
         out[:, columns(l)] = total
         return carry
 
-    lax.fori_loop(0, 2, own_leaf, 0)
+    def add(l, value):
+        out[:, columns(l)] = out[:, columns(l)] + value
+
+    lax.fori_loop(0, 1, own_leaf, 0)
+    vec_out(1)
+    lax.fori_loop(1, 2, own_leaf, 0)
+
+    lax.fori_loop(2, 3, own_leaf, 0)
+    shift(("l0", 0), l0.at[pl.ds(4, 3)], l0.at[pl.ds(0, 3)], 1)
+    shift(("l0", 1), l0.at[pl.ds(3, 3)], l0.at[pl.ds(7, 3)], -1)
 
     for copy in load_c:
         copy.wait()
@@ -298,17 +304,15 @@
     f4s[...] = far4.astype(bf16)
     for k in range(3):
         links.out(f4s, f4r.at[k], line[k], arrival(("f4", k), f4r.at[k]))
-
-    lax.fori_loop(2, 4, own_leaf, 0)
+    vec_out(2)
+
+    lax.fori_loop(3, 4, own_leaf, 0)
 
     arrive(("pts", 0), ("pts", 1))
     for w in (2, 7, 1, 8, 0, 9):
         spread(w)
         source_factors(w)
 
-    def add(l, value):
-        out[:, columns(l)] = out[:, columns(l)] + value
-
     def beside(l, carry):
         add(l, tile(l, 2))
         add(l + 1, tile(l + 1, 7))
@@ -316,6 +320,14 @@
 
     arrive(("vec", 0, 0), ("vec", 0, 1))
     lax.fori_loop(0, 3, beside, 0)
+
+    def second(l, carry):
+        add(l, tile(l, 1))
+        add(l + 2, tile(l + 2, 8))
+        return carry
+
+    arrive(("vec", 1, 0), ("vec", 1, 1))
+    lax.fori_loop(0, 2, second, 0)
 
     arrive(*[("l2", k) for k in range(4)], *[("l1", k) for k in range(4)])
     far2 = nt(l2[0], c2[0]) + nt(l2[1], c2[1]) + nt(l2[2], c2[2]) + nt(l2[3], c2[3])
@@ -323,6 +335,10 @@
     for t in range(2):
         part = nt(l1[t], c1[4 * t]) + nt(l1[1 + t], c1[4 * t + 1])
         far1.append(part + nt(l1[5 + t], c1[4 * t + 2]) + nt(l1[6 + t], c1[4 * t + 3]))
+    arrive(("l0", 0), ("l0", 1))
+    for l in range(4):
+        far = nt(l0[l], c0[4 * l]) + nt(l0[l + 1], c0[4 * l + 1])
+        far0[l] = far + nt(l0[l + 5], c0[4 * l + 2]) + nt(l0[l + 6], c0[4 * l + 3])
     arrive("f3", *[("f4", k) for k in range(3)])
     down4 = far4
     for k in range(3):
@@ -331,25 +347,26 @@
     down2 = (far2 + nt(down3.astype(bf16), e2[...])).astype(bf16)
     down1 = [(far1[t] + nt(down2, e1[t])).astype(bf16) for t in range(2)]
     for l in range(4):
-        far0[l] = nt(down1[l // 2], e0[l])
-
-    def second(l, carry):
-        add(l, tile(l, 1))
-        add(l + 2, tile(l + 2, 8))
-        return carry
-
-    arrive(("vec", 1, 0), ("vec", 1, 1))
-    lax.fori_loop(0, 2, second, 0)
+        down0 = (far0[l] + nt(down1[l // 2], e0[l])).astype(bf16)
+        add(l, nt(down0, basis[l]))
+
     arrive(("vec", 2, 0), ("vec", 2, 1))
     add(0, tile(0, 0))
     add(3, tile(3, 9))
-
-    arrive(("l0", 0), ("l0", 1))
-    for l in range(4):
-        far = far0[l] + nt(l0[l], c0[4 * l]) + nt(l0[l + 1], c0[4 * l + 1])
-        far = far + nt(l0[l + 5], c0[4 * l + 2]) + nt(l0[l + 6], c0[4 * l + 3])
-        add(l, nt(far.astype(bf16), basis[l]))
     links.drain()
+
+
+def hand_on(source, target, sem):
+    rows = source.shape[0] // COPIES
+    parts = [pl.ds(rows * k, rows) for k in range(COPIES)]
+    copies = [
+        pltpu.make_async_copy(source.at[part], target.at[part], sem.at[k])
+        for k, part in enumerate(parts)
+    ]
+    for copy in copies:
+        copy.start()
+    for copy in copies:
+        copy.wait()
 
 
 def body(size, vectors, points, basis, near_list, e0, e1, e2, e3, c0, c1, c2, c3, c4):
@@ -361,9 +378,14 @@
     def squares(count):
         return pltpu.VMEM((count, rank, rank), bf16)
 
-    return pl.pallas_call(
+    operands = (
+        vectors, points, basis, near_list,
+        e0.reshape(-1, rank, rank), e1.reshape(-1, rank, rank), e2, e3,
+        c0, c1, c2, c3, c4,
+    )
+    result = pl.pallas_call(
         functools.partial(kernel, size),
-        out_shape=jax.ShapeDtypeStruct((vecs, count), f32),
+        out_shape=pltpu.VMEM((vecs, count), f32),
         in_specs=[hbm] * 13,
         out_specs=pl.BlockSpec(memory_space=pltpu.VMEM),
         scratch_shapes=[
@@ -404,16 +426,22 @@
             pltpu.SemaphoreType.DMA((40,)),
         ],
         compiler_params=pltpu.CompilerParams(
-            collective_id=0, has_side_effects=True, vmem_limit_bytes=60 * 2**20
+            collective_id=0, has_side_effects=True, vmem_limit_bytes=40 * 2**20
         ),
         cost_estimate=pl.CostEstimate(
             flops=6_000_000_000, bytes_accessed=4_000_000, transcendentals=7_340_032
         ),
-    )(
-        vectors, points, basis, near_list,
-        e0.reshape(-1, rank, rank), e1.reshape(-1, rank, rank), e2, e3,
-        c0, c1, c2, c3, c4,
-    )
+    )(*[pltpu.with_memory_space_constraint(x, pltpu.HBM) for x in operands])
+    return pl.pallas_call(
+        hand_on,
+        out_shape=jax.ShapeDtypeStruct((vecs, count), f32),
+        in_specs=[pl.BlockSpec(memory_space=pltpu.VMEM)],
+        out_specs=hbm,
+        scratch_shapes=[
+            pltpu.SemaphoreType.DMA((COPIES,)),
+        ],
+        compiler_params=pltpu.CompilerParams(vmem_limit_bytes=16 * 2**20),
+    )(result)
 
 
 def solution(mesh):

time: 40.6 us -> 34.6 us (0.85)
  Pallas kernels: 38.1 us -> 34.5 us
  local copies, waits for them, and re-layouts: 2.3 us -> 0 us
    pallas_call x1 -> x2, Pallas kernels: 38.1 us -> 34.5 us  [the longest x1 33.4 us: body(): pl.pallas_call(functools.partial(kernel, size), out_shape=pltpu.VMEM((vec...]
    unnamed x1 -> x0, local copies, waits for them, and re-layouts: 2.3 us -> none
where the time goes in v3:
time: 34.6 us; the launch traced here: 34.5 us
  Pallas kernels  34.5 us (100%)
    pallas_call x1, Pallas kernels, body(): pl.pallas_call(functools.partial(kernel, size), out_shape=pltpu.VMEM((vec...  33.4 us
    pallas_call x1, Pallas kernels, body(): pl.pallas_call(hand_on, out_shape=jax.ShapeDtypeStruct((vecs, count), f32...  1.03 us

profile of v3, /device:TPU:384, one launch (start us, length us, event | category | flops | bytes accessed | tf_op | source)
XLA Modules:
  0.0 34.5 jit_solution(5169771283073646086)
XLA Ops:
  0.0 33.4 %shard_map.127.source = f32[128,2048]{1,0:T(8,128)S(1)} custom-call(f32[128,2048]{1,0:T(8,128)} %vec_hbm.1, bf16[3,2048]{1,0:T(4,128)(2,1)} %pts_hbm.1, bf16[2048,128]{1,0:T(8,128)(2,1)} %basis_hbm.1, s32[4,7]{1,0:T(4,128)} %near_hbm.1, bf16[4,128,128]{2,1,0:T(8,128)(2,1)} %bitcast.2, bf16[2,128,128]{2,1,0:T(8,128)(2,1)} %bitcast.3, ...), custom_call_target="tpu_custom_call" | custom-call | flops 6000000000 | bytes 4000000 | tf_op jit(solution)/shard_map/pallas_call | solution.py:386
  33.4 1.0 %shard_map.128 = f32[128,2048]{1,0:T(8,128)} custom-call(f32[128,2048]{1,0:T(8,128)S(1)} %shard_map.127.source), custom_call_target="tpu_custom_call" | custom-call | tf_op jit(solution)/shard_map/pallas_call | solution.py:435

commit v4 on v3

--- a/solution.py
+++ b/solution.py
@@ -123,12 +123,14 @@
         loads.append(copy)
         return copy
 
-    load_vec = [
-        load(vec_hbm.at[:, pl.ds(512 * l, 512)], vec_in.at[l]) for l in (3, 0, 2, 1)
-    ]
+    def load_leaf(l):
+        return load(vec_hbm.at[:, pl.ds(512 * l, 512)], vec_in.at[l])
+
+    load_vec = {l: load_leaf(l) for l in (3, 0)}
     load_pts = load(pts_hbm, pts)
     e3_rows = e3.at[pl.ds(pl.multiple_of(64 * half, 64), 64)]
     load_e3 = load(e3_hbm, e3_rows)
+    load_vec.update({l: load_leaf(l) for l in (2, 1)})
     load_basis = [
         load(basis_hbm.at[pl.ds(512 * l, 512)], basis.at[l]) for l in range(4)
     ]
@@ -153,19 +155,12 @@
         pl.when(jnp.logical_not(inside(three_from[k])))(functools.partial(clear_all, l3r.at[k]))
         pl.when(jnp.logical_not(inside(four_from[k])))(functools.partial(clear_all, l4r.at[k]))
 
-    load_pts.wait()
-    place = lax.broadcasted_iota(jnp.int32, (16, 128), 0)
-    for l in range(4):
-        x = pts[:, 512 * l : 512 * (l + 1)].astype(f32)
-        dense = jnp.zeros((16, 128), f32)
-        for k in range(3):
-            for b in range(4):
-                piece = jnp.broadcast_to(x[k : k + 1, 128 * b : 128 * (b + 1)], (16, 128))
-                dense = jnp.where(place == 4 * k + b, piece, dense)
-        ptd[3 + l] = dense.astype(bf16)
-    for copy, l in zip(load_vec, (3, 0, 2, 1), strict=True):
-        copy.wait()
+    def take_leaf(l):
+        load_vec[l].wait()
         vw[3 + l] = vec_in[l].astype(bf16)
+
+    take_leaf(3)
+    take_leaf(0)
     load_e3.wait()
 
     links = Links(send_sem, recv_sem, core)
@@ -195,9 +190,9 @@
     other_rows = e3.at[pl.ds(pl.multiple_of(64 - 64 * half, 64), 64)]
     slot = arrival("e3", other_rows)
     links.out(e3_rows, e3_rows, pair, slot)
-    shift(("pts", 0), ptd.at[pl.ds(4, 3)], ptd.at[pl.ds(0, 3)], 1)
-    shift(("pts", 1), ptd.at[pl.ds(3, 3)], ptd.at[pl.ds(7, 3)], -1)
     vec_out(0)
+    take_leaf(2)
+    take_leaf(1)
 
     for l in range(4):
         load_basis[l].wait()
@@ -222,6 +217,19 @@
     shift(("l1", 1), l1.at[pl.ds(3, 2)], l1.at[pl.ds(5, 2)], -1)
     shift(("l1", 2), l1.at[4], l1.at[0], 2)
     shift(("l1", 3), l1.at[3], l1.at[7], -2)
+
+    load_pts.wait()
+    place = lax.broadcasted_iota(jnp.int32, (16, 128), 0)
+    for l in range(4):
+        x = pts[:, 512 * l : 512 * (l + 1)].astype(f32)
+        dense = jnp.zeros((16, 128), f32)
+        for k in range(3):
+            for b in range(4):
+                piece = jnp.broadcast_to(x[k : k + 1, 128 * b : 128 * (b + 1)], (16, 128))
+                dense = jnp.where(place == 4 * k + b, piece, dense)
+        ptd[3 + l] = dense.astype(bf16)
+    shift(("pts", 0), ptd.at[pl.ds(4, 3)], ptd.at[pl.ds(0, 3)], 1)
+    shift(("pts", 1), ptd.at[pl.ds(3, 3)], ptd.at[pl.ds(7, 3)], -1)
 
     def source_factors(w):
         rows = [x3[w, pl.ds(k, 1), :] for k in range(3)]

time: 34.6 us -> 34.7 us (level)
  no operation moved by 1% of the time
where the time goes in v4:
time: 34.7 us; the launch traced here: 34.5 us
  Pallas kernels  34.5 us (99%)
    pallas_call x1, Pallas kernels, body(): pl.pallas_call(functools.partial(kernel, size), out_shape=pltpu.VMEM((vec...  33.5 us
    pallas_call x1, Pallas kernels, body(): pl.pallas_call(hand_on, out_shape=jax.ShapeDtypeStruct((vecs, count), f32...  1.03 us

profile of v4, /device:TPU:384, one launch (start us, length us, event | category | flops | bytes accessed | tf_op | source)
XLA Modules:
  0.0 34.5 jit_solution(17444168419900518603)
XLA Ops:
  0.0 33.5 %shard_map.127.source = f32[128,2048]{1,0:T(8,128)S(1)} custom-call(f32[128,2048]{1,0:T(8,128)} %vec_hbm.1, bf16[3,2048]{1,0:T(4,128)(2,1)} %pts_hbm.1, bf16[2048,128]{1,0:T(8,128)(2,1)} %basis_hbm.1, s32[4,7]{1,0:T(4,128)} %near_hbm.1, bf16[4,128,128]{2,1,0:T(8,128)(2,1)} %bitcast.2, bf16[2,128,128]{2,1,0:T(8,128)(2,1)} %bitcast.3, ...), custom_call_target="tpu_custom_call" | custom-call | flops 6000000000 | bytes 4000000 | tf_op jit(solution)/shard_map/pallas_call | solution.py:394
  33.5 1.0 %shard_map.128 = f32[128,2048]{1,0:T(8,128)} custom-call(f32[128,2048]{1,0:T(8,128)S(1)} %shard_map.127.source), custom_call_target="tpu_custom_call" | custom-call | tf_op jit(solution)/shard_map/pallas_call | solution.py:443
